TPU v7x, 32 devices: a whole 2x2x4 slice. The times are simulated.
32 devices in a mesh: dp: 16 (over z, y, x), rollout: 2 (over core).
Axes of the slice: x: 2, y: 2, z: 4, core: 2. Of those that a mesh axis runs over, the one named last changes fastest.
Arguments:
- layer_inputs: bfloat16 [2, 12288, 128], P('rollout', 'dp'), may hold values from -6 to 6
- cotangent: bfloat16 [2, 12288, 2048], P('rollout', 'dp'), may hold values from -0.0546875 to 0.0546875
- master: float32 [2, 128, 2048], P('rollout', 'dp'), may hold values from -6 to 6
- first_moment: float32 [2, 128, 2048], P('rollout', 'dp'), may hold values from -6 to 6
- second_moment: float32 [2, 128, 2048], P('rollout', 'dp'), may hold values from 0.01 to 4
- step_count: int32 [2], P('rollout'), may hold values from 1 to 1999
- bucket_owner: int32 [2], replicated, may hold values from 0 to 1, each once
Outputs:
- new_master: float32 [2, 128, 2048], P('rollout', 'dp')
- new_first: float32 [2, 128, 2048], P('rollout', 'dp')
- new_second: float32 [2, 128, 2048], P('rollout', 'dp')
- published: bfloat16 [2, 128, 2048], P(None, 'dp')
Inputs may be any that keep to these rules, and one draw needn't show every extreme that they name: `bucket_owner`: each group is named once.
All inputs are finite; a program needn't handle non-finite values.
Results may differ from a plain program's by a relative error of at most 0.001.
Values may be sent and summed in bfloat16 or wider, within the bound.
No kernel may reach another device: no remote copies, remote signals or barrier semaphores. Data moves between devices by JAX's collectives and lax.ppermute only.
A program may use at most 64 MiB of HBM per device.

v0:
```python
import jax
import jax.numpy as jnp
from jax import lax
from jax.sharding import PartitionSpec as P


def rounded_term(features, upstream):
    term = lax.dot_general(
        features, upstream, (((0,), (0,)), ((), ())), preferred_element_type=jnp.float32
    )
    return lax.optimization_barrier(term.astype(jnp.bfloat16)).astype(jnp.float32)


def per_device(
    layer_inputs, cotangent, master, first_moment, second_moment, step_count, bucket_owner
):
    features = layer_inputs[0]
    upstream = cotangent[0]
    full_grad = rounded_term(features, upstream)
    grad = lax.psum_scatter(full_grad, "dp", scatter_dimension=0, tiled=True)
    grad = grad[None]
    new_first = 0.9 * first_moment + 0.1 * grad
    new_second = 0.999 * second_moment + 0.001 * grad * grad
    counts = (step_count + 1).astype(jnp.float32)[:, None, None]
    corr_one = 1.0 - jnp.power(jnp.float32(0.9), counts)
    corr_two = 1.0 - jnp.power(jnp.float32(0.999), counts)
    update = new_first / corr_one / (jnp.sqrt(new_second / corr_two) + 1e-08) + 0.1 * master
    new_master = master - 0.02 * update
    rounded = new_master.astype(jnp.bfloat16)
    every_group = lax.all_gather(rounded, "rollout", axis=0, tiled=True)
    published = jnp.take(every_group, bucket_owner, axis=0)
    return (new_master, new_first, new_second, published)


def solution(mesh):
    in_specs = (
        P("rollout", "dp", None),
        P("rollout", "dp", None),
        P("rollout", "dp", None),
        P("rollout", "dp", None),
        P("rollout", "dp", None),
        P("rollout"),
        P(),
    )
    out_specs = (
        P("rollout", "dp", None),
        P("rollout", "dp", None),
        P("rollout", "dp", None),
        P(None, "dp", None),
    )
    return jax.shard_map(
        per_device, mesh=mesh, in_specs=in_specs, out_specs=out_specs, check_vma=False
    )
```

profile of v0, /device:TPU:0, one launch (start us, length us, event | category | flops | bytes accessed | tf_op | source)
XLA Modules:
  0.0 103.7 jit_solution(13803197029455268857)
XLA Ops:
  7.2 0.0 copy-start
  7.2 0.0 copy-start.4
  7.2 0.0 copy-start.3
  7.2 0.0 copy-start.2
  7.2 0.0 copy-start.1
  7.2 0.0 reduce-scatter.2.cloned.1.call-start
  7.3 1.8 %copy-done = bf16[1,768,2048]{2,1,0:T(8,128)(2,1)S(1)} copy-done((bf16[1,768,2048]{2,1,0:T(8,128)(2,1)S(1)}, bf16[1,768,2048]{2,1,0:T(8,128)(2,1)}, u32[]{:S(2)}) %copy-start) | copy-done | bytes 3145752
  9.1 1.5 %fusion.2 = bf16[128,2048]{1,0:T(8,128)(2,1)S(1)} fusion(bf16[1,768,2048]{2,1,0:T(8,128)(2,1)S(1)} %copy-done, bf16[1,768,128]{2,1,0:T(8,128)(2,1)} %param.7), kind=kOutput, calls=%fused_computation.3 | convolution fusion | flops 402915328 | bytes 3866624 | tf_op jit(solution)/shard_map/dot_general | solution.py:8
  10.6 1.1 %convert_element_type.13 = f32[128,2048]{1,0:T(8,128)} convert(bf16[128,2048]{1,0:T(8,128)(2,1)S(1)} %fusion.2) | non-fusion elementwise | flops 262144 | bytes 1572864 | tf_op jit(solution)/shard_map/convert_element_type | solution.py:11
  11.7 0.0 reduce-scatter.2.cloned.1.call-update
  12.4 0.0 copy-done.4
  12.5 79.8 %reduce-scatter.2.cloned.1.call-done = f32[8,2048]{1,0:T(8,128)} async-done(((f32[128,2048]{1,0:T(8,128)}), f32[8,2048]{1,0:T(8,128)}) %reduce-scatter.2.cloned.1.call-update) | async-done | bytes 65552 | tf_op jit(solution)/shard_map/reduce_scatter | solution.py:20
  92.2 0.0 copy-done.3
  92.2 0.0 copy-done.2
  92.2 0.0 copy-done.1
  92.2 1.5 %fusion.8 = (bf16[1,8,2048]{2,1,0:T(8,128)(2,1)S(1)}, f32[1,8,2048]{2,1,0:T(8,128)}, f32[1,8,2048]{2,1,0:T(8,128)}, f32[1,8,2048]{2,1,0:T(8,128)}) fusion(f32[1,8,2048]{2,1,0:T(8,128)S(1)} %copy-done.1, f32[]{:T(128)} %bitcast.5, f32[]{:T(128)} %bitcast.3, f32[8,2048]{1,0:T(8,128)} %reduce-scatter.2.cloned.1.call-done, f32[1,8,2048]{2,1,0:T(8,128)S(1)} %copy-done.2, ...), kind=kLoop, calls=%fused_computation.14 | loop fusion | flops 262144 | bytes 491528 | tf_op jit(solution)/shard_map/convert_element_type | solution.py:29
  93.8 1.8 %all_gather.3 = bf16[2,8,2048]{2,1,0:T(8,128)(2,1)S(1)} all-gather(bf16[1,8,2048]{2,1,0:T(8,128)(2,1)S(1)} %get-tuple-element.4), channel_id=1, replica_groups=mesh['dp'=16,'rollout'=2] {'rollout'}, dimensions={0}, use_global_device_ids=true | all-gather | bytes 98304 | tf_op jit(solution)/shard_map/all_gather | solution.py:30
  95.6 0.5 gather_fusion
  96.2 0.7 broadcast_select_fusion
  (3 shorter events, 0.0 us)
Async XLA Ops:
  7.2 1.9 %copy-start = (bf16[1,768,2048]{2,1,0:T(8,128)(2,1)S(1)}, bf16[1,768,2048]{2,1,0:T(8,128)(2,1)}, u32[]{:S(2)}) copy-start(bf16[1,768,2048]{2,1,0:T(8,128)(2,1)} %param.8) | copy-start | bytes 9437188
  7.2 5.2 %copy-start.4 = (s32[2]{0:T(128)S(1)}, s32[2]{0:T(128)}, u32[]{:S(2)}) copy-start(s32[2]{0:T(128)} %param.13) | copy-start | bytes 28
  7.2 85.0 %copy-start.3 = (f32[1,8,2048]{2,1,0:T(8,128)S(1)}, f32[1,8,2048]{2,1,0:T(8,128)}, u32[]{:S(2)}) copy-start(f32[1,8,2048]{2,1,0:T(8,128)} %param.10) | copy-start | bytes 196612
  7.2 85.0 %copy-start.2 = (f32[1,8,2048]{2,1,0:T(8,128)S(1)}, f32[1,8,2048]{2,1,0:T(8,128)}, u32[]{:S(2)}) copy-start(f32[1,8,2048]{2,1,0:T(8,128)} %param.11) | copy-start | bytes 196612
  7.2 85.0 %copy-start.1 = (f32[1,8,2048]{2,1,0:T(8,128)S(1)}, f32[1,8,2048]{2,1,0:T(8,128)}, u32[]{:S(2)}) copy-start(f32[1,8,2048]{2,1,0:T(8,128)} %param.9) | copy-start | bytes 196612
  7.2 85.0 %reduce-scatter.2.cloned.1.call-start = ((), (), s32[]{:S(2)}) async-start(), calls=%async_computation.1 | async-start | bytes 1114112 | tf_op jit(solution)/shard_map/reduce_scatter | solution.py:20
Sparse Core Ops, SparseCore 0:
  11.8 80.3 reduce-scatter.1
where the time goes:
time: 104 us
  waiting for transfers between devices  79.8 us (77%)
  between operations  14.8 us (14%)
  other arithmetic  3.33 us (3%)
  local copies, waits for them, and re-layouts  2.37 us (2%)
  blocking collectives  1.84 us (2%)
  matrix products  1.53 us (1%)
    reduce_scatter x1, waiting for transfers between devices, per_device(): grad = lax.psum_scatter(full_grad, 'dp', scatter_dimension=0, tiled=True)  79.8 us
  transfers between devices with their start and end apart: 1, of which 1 were waited for; matrix products, arithmetic and copies ran while one was open for 0% of the time, Pallas kernels for 0%

commit v1 on v0

v1 whole, which is shorter than its diff:
```python
import functools
import jax
import jax.numpy as jnp
from jax import lax
from jax.sharding import PartitionSpec as P


def rounded_term(features, upstream):
    term = lax.dot_general(
        features, upstream, (((0,), (0,)), ((), ())), preferred_element_type=jnp.float32
    )
    return lax.optimization_barrier(term.astype(jnp.bfloat16))


def tail(grad, master, first_moment, second_moment, step_count, bucket_owner, n_ro):
    grad = grad[None]
    new_first = 0.9 * first_moment + 0.1 * grad
    new_second = 0.999 * second_moment + 0.001 * grad * grad
    counts = (step_count + 1).astype(jnp.float32)[:, None, None]
    corr_one = 1.0 - jnp.power(jnp.float32(0.9), counts)
    corr_two = 1.0 - jnp.power(jnp.float32(0.999), counts)
    update = new_first / corr_one / (jnp.sqrt(new_second / corr_two) + 1e-08) + 0.1 * master
    new_master = master - 0.02 * update
    rounded = new_master.astype(jnp.bfloat16)
    if n_ro == 2:
        other = lax.ppermute(rounded, "rollout", [(0, 1), (1, 0)])
        mine = (bucket_owner == lax.axis_index("rollout"))[:, None, None]
        published = jnp.where(mine, rounded, other)
    else:
        every_group = lax.all_gather(rounded, "rollout", axis=0, tiled=True)
        published = jnp.take(every_group, bucket_owner, axis=0)
    return (new_master, new_first, new_second, published)

def total(blocks):
    acc = None
    for b in blocks:
        b = b.astype(jnp.float32)
        acc = b if acc is None else acc + b
    return acc

def solution(mesh):
    n_dp = mesh.shape["dp"]
    n_ro = mesh.shape["rollout"]
    def per_device(layer_inputs, cotangent, master, first_moment, second_moment, step_count, bucket_owner):
        partial = rounded_term(layer_inputs[0], cotangent[0])
        grad = reduce(partial, n_dp)
        return tail(grad, master, first_moment, second_moment, step_count, bucket_owner, n_ro)
    s = P("rollout", "dp", None)
    return jax.shard_map(
        per_device, mesh=mesh, in_specs=(s, s, s, s, s, P("rollout"), P()), out_specs=(s, s, s, P(None, "dp", None)), check_vma=False
    )
def reduce(partial, n):
    rows = partial.shape[0] // n
    r = lax.all_to_all(partial.reshape(n, rows, -1), "dp", 0, 0, tiled=True)
    return total([r[i] for i in range(n)])
```

time: 104 us -> 32.5 us (0.31)
  waiting for transfers between devices: 79.8 us -> 15.6 us
  between operations: 14.8 us -> 1.43 us
  starting transfers between devices: 0.04 us -> 8.37 us
  blocking collectives: 1.84 us -> 0 us
    reduce_scatter x1 -> x0, waiting for transfers between devices: 79.8 us -> none  [per_device(): grad = lax.psum_scatter(full_grad, 'dp', scatter_dimension=0, tiled=True)]
    all_to_all x0 -> x1, waiting for transfers between devices: none -> 14.5 us  [reduce(): r = lax.all_to_all(partial.reshape(n, rows, -1), 'dp', 0, 0, tiled=True)]
    all_to_all x0 -> x1, starting transfers between devices: none -> 8.36 us  [reduce(): r = lax.all_to_all(partial.reshape(n, rows, -1), 'dp', 0, 0, tiled=True)]
    all_gather x1 -> x0, blocking collectives: 1.84 us -> none  [per_device(): every_group = lax.all_gather(rounded, 'rollout', axis=0, tiled=True)]
    ppermute x0 -> x1, waiting for transfers between devices: none -> 1.18 us  [tail(): other = lax.ppermute(rounded, 'rollout', [(0, 1), (1, 0)])]
    convert_element_type x2 -> x1, other arithmetic: 2.61 us -> 1.77 us  [tail(): rounded = new_master.astype(jnp.bfloat16)]
  transfers between devices with their start and end apart: 1 -> 2, of which waited for: 1 -> 2; matrix products, arithmetic and copies ran while one was open for 0% -> 0% of each run, Pallas kernels for 0% -> 0%
where the time goes in v1:
time: 32.5 us; the launch traced here: 32.1 us
  waiting for transfers between devices  15.6 us (48%)
  starting transfers between devices  8.37 us (26%)
  other arithmetic  2.48 us (8%)
  matrix products  2.35 us (7%)
  local copies, waits for them, and re-layouts  1.87 us (6%)
  between operations  1.43 us (4%)
    all_to_all x1, waiting for transfers between devices, reduce(): r = lax.all_to_all(partial.reshape(n, rows, -1), 'dp', 0, 0, tiled=True)  14.5 us
    all_to_all x1, starting transfers between devices, reduce(): r = lax.all_to_all(partial.reshape(n, rows, -1), 'dp', 0, 0, tiled=True)  8.36 us
    dot_general x1, matrix products, rounded_term(): lax.dot_general(features, upstream, (((0,), (0,)), ((), ())), preferred_e...  2.35 us
    unnamed x10, local copies, waits for them, and re-layouts  1.87 us
    convert_element_type x1, other arithmetic, tail(): rounded = new_master.astype(jnp.bfloat16)  1.77 us
    ppermute x1, waiting for transfers between devices, tail(): other = lax.ppermute(rounded, 'rollout', [(0, 1), (1, 0)])  1.18 us
    select_n x1, other arithmetic, tail(): published = jnp.where(mine, rounded, other)  0.71 us
  transfers between devices with their start and end apart: 2, of which 2 were waited for; matrix products, arithmetic and copies ran while one was open for 0% of the time, Pallas kernels for 0%

profile of v1, /device:TPU:0, one launch (start us, length us, event | category | flops | bytes accessed | tf_op | source)
XLA Modules:
  0.0 32.1 jit_solution(773562356809494628)
XLA Ops:
  0.6 0.0 copy-start
  0.6 0.0 copy-start.3
  0.7 0.0 copy-start.2
  0.7 0.0 copy-start.1
  0.7 1.9 %copy-done = bf16[1,768,2048]{2,1,0:T(8,128)(2,1)S(1)} copy-done((bf16[1,768,2048]{2,1,0:T(8,128)(2,1)S(1)}, bf16[1,768,2048]{2,1,0:T(8,128)(2,1)}, u32[]{:S(2)}) %copy-start) | copy-done | bytes 3145752
  2.5 0.0 copy-start.4
  2.5 2.3 %fusion.2 = bf16[128,2048]{1,0:T(8,128)(2,1)} fusion(bf16[1,768,2048]{2,1,0:T(8,128)(2,1)S(1)} %copy-done, bf16[1,768,128]{2,1,0:T(8,128)(2,1)} %param.7), kind=kOutput, calls=%fused_computation.2 | convolution fusion | flops 402915328 | bytes 3866624 | tf_op jit(solution)/shard_map/dot_general | solution.py:9
  4.9 8.4 %all-to-all-start = ((bf16[16,8,2048]{2,1,0:T(8,128)(2,1)}), bf16[16,8,2048]{2,1,0:T(8,128)(2,1)}, u32[]{:S(2)}, u32[]{:S(2)}) async-start(bf16[16,8,2048]{2,1,0:T(8,128)(2,1)} %bitcast.13), calls=%async_computation | async-start | bytes 1048576 | tf_op jit(solution)/shard_map/all_to_all | solution.py:54
  14.0 14.5 %all-to-all-done = bf16[16,8,2048]{2,1,0:T(8,128)(2,1)} async-done(((bf16[16,8,2048]{2,1,0:T(8,128)(2,1)}), bf16[16,8,2048]{2,1,0:T(8,128)(2,1)}, u32[]{:S(2)}, u32[]{:S(2)}) %all-to-all-start) | async-done | bytes 524320 | tf_op jit(solution)/shard_map/all_to_all | solution.py:54
  28.4 0.0 copy-done.3
  28.4 0.0 copy-done.2
  28.4 0.0 copy-done.1
  28.5 1.8 %fusion.7 = (bf16[1,8,2048]{2,1,0:T(8,128)(2,1)S(1)}, f32[1,8,2048]{2,1,0:T(8,128)}, f32[1,8,2048]{2,1,0:T(8,128)}, f32[1,8,2048]{2,1,0:T(8,128)}) fusion(f32[1,8,2048]{2,1,0:T(8,128)S(1)} %copy-done.1, f32[]{:T(128)} %bitcast.4, f32[]{:T(128)} %bitcast.3, f32[1,8,2048]{2,1,0:T(8,128)S(1)} %copy-done.2, f32[1,8,2048]{2,1,0:T(8,128)S(1)} %copy-done.3, ...), kind=kLoop, calls=%fused_computation.11 | loop fusion | flops 770048 | bytes 950280 | tf_op jit(solution)/shard_map/convert_element_type | solution.py:24
  30.2 0.0 collective-permute-start
  30.2 0.0 copy-done.4
  30.3 1.2 %collective-permute-done = bf16[1,8,2048]{2,1,0:T(8,128)(2,1)S(1)} collective-permute-done((bf16[1,8,2048]{2,1,0:T(8,128)(2,1)S(1)}, bf16[1,8,2048]{2,1,0:T(8,128)(2,1)S(1)}, u32[]{:S(2)}, u32[]{:S(2)}) %collective-permute-start) | collective-permute-done | bytes 32800 | tf_op jit(solution)/shard_map/ppermute | solution.py:26
  31.4 0.7 %broadcast_select_fusion = bf16[2,8,2048]{2,1,0:T(8,128)(2,1)} fusion(pred[2]{0:T(512)(128)(4,1)S(1)} %broadcast_compare_fusion, bf16[8,2048]{1,0:T(8,128)(2,1)S(1)} %bitcast.15, bf16[8,2048]{1,0:T(8,128)(2,1)S(1)} %bitcast.14), kind=kLoop, calls=%fused_computation.9 | loop fusion | flops 32768 | bytes 131074 | tf_op jit(solution)/shard_map/jit(_where)/select_n | solution.py:28
  (1 shorter events, 0.0 us)
Async XLA Ops:
  0.6 1.9 %copy-start = (bf16[1,768,2048]{2,1,0:T(8,128)(2,1)S(1)}, bf16[1,768,2048]{2,1,0:T(8,128)(2,1)}, u32[]{:S(2)}) copy-start(bf16[1,768,2048]{2,1,0:T(8,128)(2,1)} %param.8) | copy-start | bytes 9437188
  0.6 27.8 %copy-start.3 = (f32[1,8,2048]{2,1,0:T(8,128)S(1)}, f32[1,8,2048]{2,1,0:T(8,128)}, u32[]{:S(2)}) copy-start(f32[1,8,2048]{2,1,0:T(8,128)} %param.10) | copy-start | bytes 196612
  0.7 27.8 %copy-start.2 = (f32[1,8,2048]{2,1,0:T(8,128)S(1)}, f32[1,8,2048]{2,1,0:T(8,128)}, u32[]{:S(2)}) copy-start(f32[1,8,2048]{2,1,0:T(8,128)} %param.11) | copy-start | bytes 196612
  0.7 27.8 %copy-start.1 = (f32[1,8,2048]{2,1,0:T(8,128)S(1)}, f32[1,8,2048]{2,1,0:T(8,128)}, u32[]{:S(2)}) copy-start(f32[1,8,2048]{2,1,0:T(8,128)} %param.9) | copy-start | bytes 196612
  2.5 27.7 %copy-start.4 = (s32[2]{0:T(128)S(1)}, s32[2]{0:T(128)}, u32[]{:S(2)}) copy-start(s32[2]{0:T(128)} %param.13) | copy-start | bytes 28
  4.9 23.6 %all-to-all-start = ((bf16[16,8,2048]{2,1,0:T(8,128)(2,1)}), bf16[16,8,2048]{2,1,0:T(8,128)(2,1)}, u32[]{:S(2)}, u32[]{:S(2)}) async-start(bf16[16,8,2048]{2,1,0:T(8,128)(2,1)} %bitcast.13), calls=%async_computation | async-start | bytes 1048576 | tf_op jit(solution)/shard_map/all_to_all | solution.py:54
  30.2 1.2 %collective-permute-start = (bf16[1,8,2048]{2,1,0:T(8,128)(2,1)S(1)}, bf16[1,8,2048]{2,1,0:T(8,128)(2,1)S(1)}, u32[]{:S(2)}, u32[]{:S(2)}) collective-permute-start(bf16[1,8,2048]{2,1,0:T(8,128)(2,1)S(1)} %get-tuple-element.4), channel_id=1, source_target_pairs={{0,1},{1,0},{2,3},{3,2},{4,5},{5,4},{6,7},{7,6},{8,9},{9,8},{10,11... | collective-permute-start | bytes 98312 | tf_op jit(solution)/shard_map/ppermute | solution.py:26

commit v2 on v1

v2 whole, which is shorter than its diff:
```python
import functools
import jax
import jax.numpy as jnp
from jax import lax
from jax.experimental import pallas as pl
from jax.experimental.pallas import tpu as pltpu
from jax.sharding import PartitionSpec as P

VMEM_SPEC = pl.BlockSpec(memory_space=pltpu.VMEM)


def product_kernel(inner, outer, chunks, features_hbm, upstream_hbm, *refs):
    blocks, (features_ref, upstream, product, sems) = refs[:inner], refs[inner:]
    ff = upstream.shape[1]
    width = ff // chunks
    rows = product.shape[0] // (inner * outer)
    first = pltpu.make_async_copy(features_hbm, features_ref, sems.at[chunks])
    first.start()
    copies = []
    for c in range(chunks):
        cols = pl.ds(c * width, width)
        copy = pltpu.make_async_copy(upstream_hbm.at[:, cols], upstream.at[:, cols], sems.at[c])
        copy.start()
        copies.append(copy)
    mine = lax.rem(lax.axis_index("dp"), inner)
    first.wait()
    for c in range(chunks):
        cols = slice(c * width, (c + 1) * width)
        copies[c].wait()
        product[:, cols] = lax.dot_general(
            features_ref[...], upstream[:, cols], (((0,), (0,)), ((), ())), preferred_element_type=jnp.float32
        )
        for d in range(inner):
            peer = jnp.bitwise_xor(mine, d)
            parts = [
                product[pl.ds(pl.multiple_of((o * inner + peer) * rows, rows), rows), cols] for o in range(outer)
            ]
            blocks[d][:, cols] = jnp.concatenate(parts, axis=0).astype(jnp.bfloat16)


def product_blocks(features, upstream, inner, outer):
    tokens, rows = features.shape
    ff = upstream.shape[1]
    chunks = 2 if ff % 256 == 0 else 1
    block = pltpu.VMEM((rows // inner, ff), jnp.bfloat16)
    return pl.pallas_call(
        functools.partial(product_kernel, inner, outer, chunks),
        out_shape=[block] * inner,
        in_specs=[pl.BlockSpec(memory_space=pltpu.HBM)] * 2,
        out_specs=[VMEM_SPEC] * inner,
        scratch_shapes=[
            pltpu.VMEM((tokens, rows), jnp.bfloat16),
            pltpu.VMEM((tokens, ff), jnp.bfloat16),
            pltpu.VMEM((rows, ff), jnp.float32),
            pltpu.SemaphoreType.DMA((chunks + 1,)),
        ],
        compiler_params=pltpu.CompilerParams(vmem_limit_bytes=24 * 2**20),
        name="product",
    )(*(pltpu.with_memory_space_constraint(x, pltpu.HBM) for x in (features, upstream)))


def middle_kernel(inner, outer, *refs):
    got, sent, total = refs[:inner], refs[inner : inner + outer], refs[-1]
    acc = got[0][...].astype(jnp.float32)
    for g in got[1:]:
        acc = acc + g[...].astype(jnp.float32)
    total[...] = acc
    rows = total.shape[0] // outer
    mine = lax.axis_index("dp") // inner
    for d in range(outer):
        peer = jnp.bitwise_xor(mine, d)
        sent[d][...] = total[pl.ds(pl.multiple_of(peer * rows, rows), rows), :].astype(sent[d].dtype)


def middle_sums(got, inner, outer):
    rows, ff = got[0].shape
    part = pltpu.VMEM((rows // outer, ff), jnp.float32)
    got = [pltpu.with_memory_space_constraint(g, pltpu.VMEM) for g in got]
    return pl.pallas_call(
        functools.partial(middle_kernel, inner, outer),
        out_shape=[part] * outer,
        in_specs=[VMEM_SPEC] * inner,
        out_specs=[VMEM_SPEC] * outer,
        scratch_shapes=[pltpu.VMEM((rows, ff), jnp.float32)],
        compiler_params=pltpu.CompilerParams(vmem_limit_bytes=8 * 2**20),
        name="middle",
    )(*got)


def total(blocks):
    acc = None
    for b in blocks:
        b = b.astype(jnp.float32)
        acc = b if acc is None else acc + b
    return acc


def split_of(n):
    inner = 1
    while inner * inner < n:
        inner *= 2
    return inner, n // inner


def swap(blocks, stride, n):
    far = len(blocks) - 1
    got = {0: blocks[0]}
    for d in [far, *range(1, far)]:
        got[d] = lax.ppermute(blocks[d], "dp", [(i, i ^ (d * stride)) for i in range(n)])
    return list(got.values())


def solution(mesh):
    n_dp = mesh.shape["dp"]
    n_ro = mesh.shape["rollout"]

    def per_device(layer_inputs, cotangent, master, first_moment, second_moment, step_count, bucket_owner):
        inner, outer = split_of(n_dp)
        blocks = product_blocks(layer_inputs[0], cotangent[0], inner, outer)
        parts = middle_sums(swap(blocks, 1, n_dp), inner, outer)
        grad = total(swap(parts, inner, n_dp))
        return tail(grad, master, first_moment, second_moment, step_count, bucket_owner, n_ro)

    s = P("rollout", "dp", None)
    return jax.shard_map(
        per_device, mesh=mesh, in_specs=(s, s, s, s, s, P("rollout"), P()), out_specs=(s, s, s, P(None, "dp", None)), check_vma=False
    )


def tail(grad, master, first_moment, second_moment, step_count, bucket_owner, n_ro):
    grad = grad[None]
    new_first = 0.9 * first_moment + 0.1 * grad
    new_second = 0.999 * second_moment + 0.001 * grad * grad
    counts = (step_count + 1).astype(jnp.float32)[:, None, None]
    corr_one = 1.0 - jnp.power(jnp.float32(0.9), counts)
    corr_two = 1.0 - jnp.power(jnp.float32(0.999), counts)
    update = new_first / corr_one / (jnp.sqrt(new_second / corr_two) + 1e-08) + 0.1 * master
    new_master = master - 0.02 * update
    rounded = new_master.astype(jnp.bfloat16)
    if n_ro == 2:
        other = lax.ppermute(rounded, "rollout", [(0, 1), (1, 0)])
        mine = (bucket_owner == lax.axis_index("rollout"))[:, None, None]
        published = jnp.where(mine, rounded, other)
    else:
        every_group = lax.all_gather(rounded, "rollout", axis=0, tiled=True)
        published = jnp.take(every_group, bucket_owner, axis=0)
    return (new_master, new_first, new_second, published)
```

time: 32.5 us -> 25.4 us (0.78)
  waiting for transfers between devices: 15.6 us -> 10.8 us
  Pallas kernels: 0 us -> 2.6 us
  matrix products: 2.35 us -> 0 us
  local copies, waits for them, and re-layouts: 1.87 us -> 0.02 us
  other arithmetic: 2.48 us -> 1.42 us
  starting transfers between devices: 8.37 us -> 9.07 us
    all_to_all x1 -> x0, waiting for transfers between devices: 14.5 us -> none  [reduce(): r = lax.all_to_all(partial.reshape(n, rows, -1), 'dp', 0, 0, tiled=True)]
    ppermute x0 -> x6, waiting for transfers between devices: none -> 9.56 us  [swap(): lax.ppermute(blocks[d], 'dp', [(i, i ^ d * stride) for i in range(n)])]
    ppermute x0 -> x6, starting transfers between devices: none -> 9.06 us  [swap(): lax.ppermute(blocks[d], 'dp', [(i, i ^ d * stride) for i in range(n)])]
    all_to_all x1 -> x0, starting transfers between devices: 8.36 us -> none  [reduce(): r = lax.all_to_all(partial.reshape(n, rows, -1), 'dp', 0, 0, tiled=True)]
    pallas_call x0 -> x2, Pallas kernels: none -> 2.6 us  [the longest x1 2.51 us: product_blocks(): pl.pallas_call(functools.partial(product_kernel, inner, outer, chunks), o...]
    dot_general x1 -> x0, matrix products: 2.35 us -> none  [rounded_term(): lax.dot_general(features, upstream, (((0,), (0,)), ((), ())), preferred_e...]
    unnamed x10 -> x8, local copies, waits for them, and re-layouts: 1.87 us -> 0.02 us
    convert_element_type x1, other arithmetic: 1.77 us -> 0.71 us  [tail(): rounded = new_master.astype(jnp.bfloat16)]
  transfers between devices with their start and end apart: 2 -> 7, of which waited for: 2 -> 6; matrix products, arithmetic and copies ran while one was open for 0% -> 0% of each run, Pallas kernels for 0% -> 0%
where the time goes in v2:
time: 25.4 us; the launch traced here: 25.3 us
  waiting for transfers between devices  10.8 us (43%)
  starting transfers between devices  9.07 us (36%)
  Pallas kernels  2.6 us (10%)
  between operations  1.43 us (6%)
  other arithmetic  1.42 us (6%)
    ppermute x6, waiting for transfers between devices, swap(): lax.ppermute(blocks[d], 'dp', [(i, i ^ d * stride) for i in range(n)])  9.56 us
    ppermute x6, starting transfers between devices, swap(): lax.ppermute(blocks[d], 'dp', [(i, i ^ d * stride) for i in range(n)])  9.06 us
    pallas_call x1, Pallas kernels, product_blocks(): pl.pallas_call(functools.partial(product_kernel, inner, outer, chunks), o...  2.51 us
    ppermute x1, waiting for transfers between devices, tail(): other = lax.ppermute(rounded, 'rollout', [(0, 1), (1, 0)])  1.19 us
    convert_element_type x1, other arithmetic, tail(): rounded = new_master.astype(jnp.bfloat16)  0.71 us
    select_n x1, other arithmetic, tail(): published = jnp.where(mine, rounded, other)  0.71 us
  transfers between devices with their start and end apart: 7, of which 6 were waited for; matrix products, arithmetic and copies ran while one was open for 0% of the time, Pallas kernels for 0%

profile of v2, /device:TPU:0, one launch (start us, length us, event | category | flops | bytes accessed | tf_op | source)
XLA Modules:
  0.0 25.3 jit_solution(13471465075123589964)
XLA Ops:
  0.6 0.0 copy-start.2
  0.6 0.0 copy-start.1
  0.7 0.0 copy-start
  0.7 0.0 copy-start.3
  0.7 2.5 %product.1 = (bf16[32,2048]{1,0:T(8,128)(2,1)S(1)}, bf16[32,2048]{1,0:T(8,128)(2,1)S(1)}, bf16[32,2048]{1,0:T(8,128)(2,1)S(1)}, bf16[32,2048]{1,0:T(8,128)(2,1)S(1)}) custom-call(bf16[768,128]{1,0:T(8,128)(2,1)} %bitcast.15, bf16[768,2048]{1,0:T(8,128)(2,1)} %bitcast.14), custom_call_target="tpu_custom_call" | custom-call | tf_op jit(solution)/shard_map/product/pallas_call | solution.py:46
  3.2 4.0 %collective-permute-start = (bf16[32,2048]{1,0:T(8,128)(2,1)S(1)}, bf16[32,2048]{1,0:T(8,128)(2,1)S(1)}, u32[]{:S(2)}, u32[]{:S(2)}) collective-permute-start(bf16[32,2048]{1,0:T(8,128)(2,1)S(1)} %get-tuple-element.13), channel_id=1, source_target_pairs={{0,6},{2,4},{4,2},{6,0},{8,14},{10,12},{12,10},{14,8},{16,22},{18,... | collective-permute-start | bytes 393224 | tf_op jit(solution)/shard_map/ppermute | solution.py:109
  7.2 0.5 %collective-permute-start.1 = (bf16[32,2048]{1,0:T(8,128)(2,1)S(1)}, bf16[32,2048]{1,0:T(8,128)(2,1)S(1)}, u32[]{:S(2)}, u32[]{:S(2)}) collective-permute-start(bf16[32,2048]{1,0:T(8,128)(2,1)S(1)} %get-tuple-element.14), channel_id=1, source_target_pairs={{0,2},{2,0},{4,6},{6,4},{8,10},{10,8},{12,14},{14,12},{16,18},{18,... | collective-permute-start | bytes 393224 | tf_op jit(solution)/shard_map/ppermute | solution.py:109
  7.7 0.1 collective-permute-start.2
  7.8 3.7 %collective-permute-done.refs_1_ = bf16[32,2048]{1,0:T(8,128)(2,1)S(1)} collective-permute-done((bf16[32,2048]{1,0:T(8,128)(2,1)S(1)}, bf16[32,2048]{1,0:T(8,128)(2,1)S(1)}, u32[]{:S(2)}, u32[]{:S(2)}) %collective-permute-start) | collective-permute-done | bytes 131104 | tf_op jit(solution)/shard_map/ppermute | solution.py:109
  11.5 2.2 %collective-permute-done.1.refs_2_ = bf16[32,2048]{1,0:T(8,128)(2,1)S(1)} collective-permute-done((bf16[32,2048]{1,0:T(8,128)(2,1)S(1)}, bf16[32,2048]{1,0:T(8,128)(2,1)S(1)}, u32[]{:S(2)}, u32[]{:S(2)}) %collective-permute-start.1) | collective-permute-done | bytes 131104 | tf_op jit(solution)/shard_map/ppermute | solution.py:109
  13.7 0.0 collective-permute-done.2.refs_3_
  13.7 0.1 middle.1
  13.8 3.7 %collective-permute-start.3 = (f32[8,2048]{1,0:T(8,128)S(1)}, f32[8,2048]{1,0:T(8,128)S(1)}, u32[]{:S(2)}, u32[]{:S(2)}) collective-permute-start(f32[8,2048]{1,0:T(8,128)S(1)} %get-tuple-element.17), channel_id=1, source_target_pairs={{0,24},{2,26},{4,28},{6,30},{8,16},{10,18},{12,20},{14,22},{16,8},... | collective-permute-start | bytes 196616 | tf_op jit(solution)/shard_map/ppermute | solution.py:109
  17.5 0.0 collective-permute-start.4
  17.5 0.8 %collective-permute-start.5 = (f32[8,2048]{1,0:T(8,128)S(1)}, f32[8,2048]{1,0:T(8,128)S(1)}, u32[]{:S(2)}, u32[]{:S(2)}) collective-permute-start(f32[8,2048]{1,0:T(8,128)S(1)} %get-tuple-element.19), channel_id=1, source_target_pairs={{0,16},{2,18},{4,20},{6,22},{8,24},{10,26},{12,28},{14,30},{16,0},... | collective-permute-start | bytes 196616 | tf_op jit(solution)/shard_map/ppermute | solution.py:109
  19.0 1.0 %collective-permute-done.3 = f32[8,2048]{1,0:T(8,128)S(1)} collective-permute-done((f32[8,2048]{1,0:T(8,128)S(1)}, f32[8,2048]{1,0:T(8,128)S(1)}, u32[]{:S(2)}, u32[]{:S(2)}) %collective-permute-start.3) | collective-permute-done | bytes 65568 | tf_op jit(solution)/shard_map/ppermute | solution.py:109
  20.0 1.8 %collective-permute-done.4 = f32[8,2048]{1,0:T(8,128)S(1)} collective-permute-done((f32[8,2048]{1,0:T(8,128)S(1)}, f32[8,2048]{1,0:T(8,128)S(1)}, u32[]{:S(2)}, u32[]{:S(2)}) %collective-permute-start.4) | collective-permute-done | bytes 65568 | tf_op jit(solution)/shard_map/ppermute | solution.py:109
  21.8 0.9 %collective-permute-done.5 = f32[8,2048]{1,0:T(8,128)S(1)} collective-permute-done((f32[8,2048]{1,0:T(8,128)S(1)}, f32[8,2048]{1,0:T(8,128)S(1)}, u32[]{:S(2)}, u32[]{:S(2)}) %collective-permute-start.5) | collective-permute-done | bytes 65568 | tf_op jit(solution)/shard_map/ppermute | solution.py:109
  22.7 0.0 copy-done.2
  22.7 0.0 copy-done
  22.7 0.7 %fusion.2 = (bf16[1,8,2048]{2,1,0:T(8,128)(2,1)S(1)}, f32[1,8,2048]{2,1,0:T(8,128)}, f32[1,8,2048]{2,1,0:T(8,128)}, f32[1,8,2048]{2,1,0:T(8,128)}) fusion(f32[1,8,2048]{2,1,0:T(8,128)S(1)} %copy-done, f32[]{:T(128)} %bitcast.5, f32[]{:T(128)} %bitcast.3, f32[1,8,2048]{2,1,0:T(8,128)S(1)} %copy-done.1, f32[1,8,2048]{2,1,0:T(8,128)S(1)} %copy-done.2, ...), kind=kLoop, calls=%fused_computation.8 | loop fusion | flops 311296 | bytes 688136 | tf_op jit(solution)/shard_map/convert_element_type | solution.py:139
  23.4 0.0 collective-permute-start.6
  23.4 1.2 %collective-permute-done.6 = bf16[1,8,2048]{2,1,0:T(8,128)(2,1)S(1)} collective-permute-done((bf16[1,8,2048]{2,1,0:T(8,128)(2,1)S(1)}, bf16[1,8,2048]{2,1,0:T(8,128)(2,1)S(1)}, u32[]{:S(2)}, u32[]{:S(2)}) %collective-permute-start.6) | collective-permute-done | bytes 32800 | tf_op jit(solution)/shard_map/ppermute | solution.py:141
  24.6 0.7 %broadcast_select_fusion = bf16[2,8,2048]{2,1,0:T(8,128)(2,1)} fusion(pred[2]{0:T(512)(128)(4,1)S(1)} %broadcast_compare_fusion, bf16[8,2048]{1,0:T(8,128)(2,1)S(1)} %bitcast.17, bf16[8,2048]{1,0:T(8,128)(2,1)S(1)} %bitcast.16), kind=kLoop, calls=%fused_computation.6 | loop fusion | flops 32768 | bytes 131074 | tf_op jit(solution)/shard_map/jit(_where)/select_n | solution.py:143
  (3 shorter events, 0.0 us)
Async XLA Ops:
  0.6 22.0 %copy-start.2 = (f32[1,8,2048]{2,1,0:T(8,128)S(1)}, f32[1,8,2048]{2,1,0:T(8,128)}, u32[]{:S(2)}) copy-start(f32[1,8,2048]{2,1,0:T(8,128)} %param.10) | copy-start | bytes 196612
  0.6 22.0 %copy-start.1 = (f32[1,8,2048]{2,1,0:T(8,128)S(1)}, f32[1,8,2048]{2,1,0:T(8,128)}, u32[]{:S(2)}) copy-start(f32[1,8,2048]{2,1,0:T(8,128)} %param.11) | copy-start | bytes 196612
  0.7 22.0 %copy-start = (f32[1,8,2048]{2,1,0:T(8,128)S(1)}, f32[1,8,2048]{2,1,0:T(8,128)}, u32[]{:S(2)}) copy-start(f32[1,8,2048]{2,1,0:T(8,128)} %param.9) | copy-start | bytes 196612
  0.7 22.7 %copy-start.3 = (s32[2]{0:T(128)S(1)}, s32[2]{0:T(128)}, u32[]{:S(2)}) copy-start(s32[2]{0:T(128)} %param.13) | copy-start | bytes 28
  3.2 8.3 %collective-permute-start = (bf16[32,2048]{1,0:T(8,128)(2,1)S(1)}, bf16[32,2048]{1,0:T(8,128)(2,1)S(1)}, u32[]{:S(2)}, u32[]{:S(2)}) collective-permute-start(bf16[32,2048]{1,0:T(8,128)(2,1)S(1)} %get-tuple-element.13), channel_id=1, source_target_pairs={{0,6},{2,4},{4,2},{6,0},{8,14},{10,12},{12,10},{14,8},{16,22},{18,... | collective-permute-start | bytes 393224 | tf_op jit(solution)/shard_map/ppermute | solution.py:109
  7.2 6.6 %collective-permute-start.1 = (bf16[32,2048]{1,0:T(8,128)(2,1)S(1)}, bf16[32,2048]{1,0:T(8,128)(2,1)S(1)}, u32[]{:S(2)}, u32[]{:S(2)}) collective-permute-start(bf16[32,2048]{1,0:T(8,128)(2,1)S(1)} %get-tuple-element.14), channel_id=1, source_target_pairs={{0,2},{2,0},{4,6},{6,4},{8,10},{10,8},{12,14},{14,12},{16,18},{18,... | collective-permute-start | bytes 393224 | tf_op jit(solution)/shard_map/ppermute | solution.py:109
  7.7 6.0 %collective-permute-start.2 = (bf16[32,2048]{1,0:T(8,128)(2,1)S(1)}, bf16[32,2048]{1,0:T(8,128)(2,1)S(1)}, u32[]{:S(2)}, u32[]{:S(2)}) collective-permute-start(bf16[32,2048]{1,0:T(8,128)(2,1)S(1)} %get-tuple-element.15), channel_id=1, source_target_pairs={{0,4},{2,6},{4,0},{6,2},{8,12},{10,14},{12,8},{14,10},{16,20},{18,... | collective-permute-start | bytes 393224 | tf_op jit(solution)/shard_map/ppermute | solution.py:109
  13.8 6.2 %collective-permute-start.3 = (f32[8,2048]{1,0:T(8,128)S(1)}, f32[8,2048]{1,0:T(8,128)S(1)}, u32[]{:S(2)}, u32[]{:S(2)}) collective-permute-start(f32[8,2048]{1,0:T(8,128)S(1)} %get-tuple-element.17), channel_id=1, source_target_pairs={{0,24},{2,26},{4,28},{6,30},{8,16},{10,18},{12,20},{14,22},{16,8},... | collective-permute-start | bytes 196616 | tf_op jit(solution)/shard_map/ppermute | solution.py:109
  17.5 4.3 %collective-permute-start.4 = (f32[8,2048]{1,0:T(8,128)S(1)}, f32[8,2048]{1,0:T(8,128)S(1)}, u32[]{:S(2)}, u32[]{:S(2)}) collective-permute-start(f32[8,2048]{1,0:T(8,128)S(1)} %get-tuple-element.18), channel_id=1, source_target_pairs={{0,8},{2,10},{4,12},{6,14},{8,0},{10,2},{12,4},{14,6},{16,24},{18,... | collective-permute-start | bytes 196616 | tf_op jit(solution)/shard_map/ppermute | solution.py:109
  17.5 5.2 %collective-permute-start.5 = (f32[8,2048]{1,0:T(8,128)S(1)}, f32[8,2048]{1,0:T(8,128)S(1)}, u32[]{:S(2)}, u32[]{:S(2)}) collective-permute-start(f32[8,2048]{1,0:T(8,128)S(1)} %get-tuple-element.19), channel_id=1, source_target_pairs={{0,16},{2,18},{4,20},{6,22},{8,24},{10,26},{12,28},{14,30},{16,0},... | collective-permute-start | bytes 196616 | tf_op jit(solution)/shard_map/ppermute | solution.py:109
  23.4 1.2 %collective-permute-start.6 = (bf16[1,8,2048]{2,1,0:T(8,128)(2,1)S(1)}, bf16[1,8,2048]{2,1,0:T(8,128)(2,1)S(1)}, u32[]{:S(2)}, u32[]{:S(2)}) collective-permute-start(bf16[1,8,2048]{2,1,0:T(8,128)(2,1)S(1)} %get-tuple-element.20), channel_id=1, source_target_pairs={{0,1},{1,0},{2,3},{3,2},{4,5},{5,4},{6,7},{7,6},{8,9},{9,8},{10,11... | collective-permute-start | bytes 98312 | tf_op jit(solution)/shard_map/ppermute | solution.py:141

commit v3 on v2

v3 whole, which is shorter than its diff:
```python
import functools
import jax
import jax.numpy as jnp
from jax import lax
from jax.experimental import pallas as pl
from jax.experimental.pallas import tpu as pltpu
from jax.sharding import PartitionSpec as P

VMEM_SPEC = pl.BlockSpec(memory_space=pltpu.VMEM)


def turned_here(inner, outer):
    return (lax.axis_index("rollout") % 2 == 1) if inner == outer else (lax.axis_index("rollout") < 0)


def distance(step, count):
    return 0 if step == 0 else (step + count - 3) % (count - 1) + 1


def product_kernel(inner, outer, chunks, features_hbm, upstream_hbm, *refs):
    blocks, (features, upstream, product, sems) = refs[:inner], refs[inner:]
    depth = upstream.shape[0] // chunks
    rows = product.shape[0] // (inner * outer)
    copies = []
    for c in range(chunks):
        part = pl.ds(c * depth, depth)
        pair = (
            pltpu.make_async_copy(features_hbm.at[part], features.at[part], sems.at[c, 0]),
            pltpu.make_async_copy(upstream_hbm.at[part], upstream.at[part], sems.at[c, 1]),
        )
        for copy in pair:
            copy.start()
        copies.append(pair)
    turned = turned_here(inner, outer)
    mine = jnp.where(turned, lax.axis_index("dp") // inner, lax.rem(lax.axis_index("dp"), inner))
    peer_step = jnp.where(turned, inner, 1)
    other_step = jnp.where(turned, 1, inner)
    for c in range(chunks):
        part = slice(c * depth, (c + 1) * depth)
        for copy in copies[c]:
            copy.wait()
        term = lax.dot_general(
            features[part], upstream[part], (((0,), (0,)), ((), ())), preferred_element_type=jnp.float32
        )
        product[...] = term if c == 0 else product[...] + term
    for d in range(inner):
        peer = jnp.bitwise_xor(mine, distance(d, inner))
        for o in range(0, outer, 2):
            places = [((o + i) * other_step + peer * peer_step) * rows for i in range(2)]
            parts = [product[pl.ds(pl.multiple_of(at, rows), rows), :] for at in places]
            blocks[d][o * rows : (o + 2) * rows] = jnp.concatenate(parts, axis=0).astype(jnp.bfloat16)


def product_blocks(features, upstream, inner, outer):
    tokens, rows = features.shape
    ff = upstream.shape[1]
    chunks = 3 if tokens % 384 == 0 else 1
    block = pltpu.VMEM((rows // inner, ff), jnp.bfloat16)
    return pl.pallas_call(
        functools.partial(product_kernel, inner, outer, chunks),
        out_shape=[block] * inner,
        in_specs=[pl.BlockSpec(memory_space=pltpu.HBM)] * 2,
        out_specs=[VMEM_SPEC] * inner,
        scratch_shapes=[
            pltpu.VMEM((tokens, rows), jnp.bfloat16),
            pltpu.VMEM((tokens, ff), jnp.bfloat16),
            pltpu.VMEM((rows, ff), jnp.float32),
            pltpu.SemaphoreType.DMA((chunks, 2)),
        ],
        compiler_params=pltpu.CompilerParams(vmem_limit_bytes=24 * 2**20),
        name="product",
    )(*(pltpu.with_memory_space_constraint(x, pltpu.HBM) for x in (features, upstream)))


def middle_kernel(inner, outer, *refs):
    got, sent, total = refs[:inner], refs[inner : inner + outer], refs[-1]
    acc = got[0][...].astype(jnp.float32)
    for g in got[1:]:
        acc = acc + g[...].astype(jnp.float32)
    total[...] = acc
    rows = total.shape[0] // outer
    turned = turned_here(inner, outer)
    mine = jnp.where(turned, lax.rem(lax.axis_index("dp"), inner), lax.axis_index("dp") // inner)
    for d in range(outer):
        peer = jnp.bitwise_xor(mine, distance(d, outer))
        sent[d][...] = total[pl.ds(pl.multiple_of(peer * rows, rows), rows), :].astype(sent[d].dtype)


def middle_sums(got, inner, outer):
    rows, ff = got[0].shape
    part = pltpu.VMEM((rows // outer, ff), jnp.float32)
    got = [pltpu.with_memory_space_constraint(g, pltpu.VMEM) for g in got]
    return pl.pallas_call(
        functools.partial(middle_kernel, inner, outer),
        out_shape=[part] * outer,
        in_specs=[VMEM_SPEC] * inner,
        out_specs=[VMEM_SPEC] * outer,
        scratch_shapes=[pltpu.VMEM((rows, ff), jnp.float32)],
        compiler_params=pltpu.CompilerParams(vmem_limit_bytes=8 * 2**20),
        name="middle",
    )(*got)


def stepped(grad, first, second, master, step):
    new_first = 0.9 * first[0] + 0.1 * grad
    new_second = 0.999 * second[0] + 0.001 * grad * grad
    update = new_first / step[0] / (jnp.sqrt(new_second / step[1]) + 1e-08) + 0.1 * master[0]
    return master[0] - 0.02 * update, new_first, new_second


def publish_kernel(n_parts, *refs):
    parts, state, (grad, rounded) = refs[:n_parts], refs[n_parts:-2], refs[-2:]
    acc = parts[0][...].astype(jnp.float32)
    for p in parts[1:]:
        acc = acc + p[...].astype(jnp.float32)
    grad[...] = acc
    rounded[0] = stepped(acc, *state)[0].astype(jnp.bfloat16)


def store_kernel(grad, first, second, master, step, *refs):
    outs, (held, sems) = refs[:3], refs[3:]
    copies = []
    for k, value in enumerate(stepped(grad[...], first, second, master, step)):
        held[k] = value
        copy = pltpu.make_async_copy(held.at[k], outs[k].at[0], sems.at[k])
        copy.start()
        copies.append(copy)
    for copy in copies:
        copy.wait()


def held_in_vmem(arrays):
    return [pltpu.with_memory_space_constraint(x, pltpu.VMEM) for x in arrays]


def to_publish(parts, state):
    shape = state[0].shape
    args = held_in_vmem((*parts, *state))
    return pl.pallas_call(
        functools.partial(publish_kernel, len(parts)),
        out_shape=[pltpu.VMEM(shape[1:], jnp.float32), pltpu.VMEM(shape, jnp.bfloat16)],
        in_specs=[VMEM_SPEC] * len(args),
        out_specs=[VMEM_SPEC] * 2,
        compiler_params=pltpu.CompilerParams(vmem_limit_bytes=8 * 2**20),
        name="publish",
    )(*args)


def stored(grad, state):
    shape = state[0].shape
    args = held_in_vmem((grad, *state))
    return pl.pallas_call(
        store_kernel,
        out_shape=[jax.ShapeDtypeStruct(shape, jnp.float32)] * 3,
        in_specs=[VMEM_SPEC] * len(args),
        out_specs=[pl.BlockSpec(memory_space=pltpu.HBM)] * 3,
        scratch_shapes=[pltpu.VMEM((3, *shape[1:]), jnp.float32), pltpu.SemaphoreType.DMA((3,))],
        compiler_params=pltpu.CompilerParams(vmem_limit_bytes=8 * 2**20),
        cost_estimate=pl.CostEstimate(flops=2**20, bytes_accessed=2**20, transcendentals=0),
        name="store",
    )(*args)


def split_of(n):
    inner = 1
    while inner * inner < n:
        inner *= 2
    return inner, n // inner


def swap(blocks, strides, n, n_ro):
    count = len(blocks)
    got = [blocks[0]]
    for step in range(1, count):
        pairs = []
        for i in range(n):
            for r in range(n_ro):
                turned = r % 2 if strides[0] != strides[1] else 0
                pairs.append((i * n_ro + r, (i ^ (distance(step, count) * strides[turned])) * n_ro + r))
        got.append(lax.ppermute(blocks[step], ("dp", "rollout"), pairs))
    return got


def solution(mesh):
    n_dp = mesh.shape["dp"]
    n_ro = mesh.shape["rollout"]

    def per_device(layer_inputs, cotangent, master, first_moment, second_moment, step_count, bucket_owner):
        inner, outer = split_of(n_dp)
        strides = (1, inner) if inner == outer else (1, 1)
        blocks = product_blocks(layer_inputs[0], cotangent[0], inner, outer)
        parts = middle_sums(swap(blocks, strides, n_dp, n_ro), inner, outer)
        counts = (step_count + 1).astype(jnp.float32)
        corrections = 1.0 - jnp.power(jnp.array([0.9, 0.999], jnp.float32), counts)
        state = (first_moment, second_moment, master, corrections[:, None, None])
        grad, rounded = to_publish(swap(parts, strides[::-1], n_dp, n_ro), state)
        new_master, new_first, new_second = stored(grad, state)
        if n_ro == 2:
            other = lax.ppermute(rounded, "rollout", [(0, 1), (1, 0)])
            published = jnp.where((bucket_owner == lax.axis_index("rollout"))[:, None, None], rounded, other)
        else:
            every_group = lax.all_gather(rounded, "rollout", axis=0, tiled=True)
            published = jnp.take(every_group, bucket_owner, axis=0)
        return new_master, new_first, new_second, published

    s = P("rollout", "dp", None)
    return jax.shard_map(
        per_device, mesh=mesh, in_specs=(s, s, s, s, s, P("rollout"), P()), out_specs=(s, s, s, P(None, "dp", None)), check_vma=False
    )
```

time: 25.4 us -> 23.8 us (0.937)
  waiting for transfers between devices: 10.8 us -> 8.81 us
  Pallas kernels: 2.6 us -> 3.46 us
  other arithmetic: 1.42 us -> 0.73 us
    ppermute x7, waiting for transfers between devices: 10.8 us -> 8.81 us  [the longest x6 8.46 us: swap(): got.append(lax.ppermute(blocks[step], ('dp', 'rollout'), pairs))]
    pallas_call x0 -> x2, Pallas kernels: none -> 0.92 us  [the longest x1 0.81 us: stored(): pl.pallas_call(store_kernel, out_shape=[jax.ShapeDtypeStruct(shape, jnp.f...]
    convert_element_type x1 -> x0, other arithmetic: 0.71 us -> none  [tail(): rounded = new_master.astype(jnp.bfloat16)]
  transfers between devices with their start and end apart: 7 -> 7, of which waited for: 6 -> 7; matrix products, arithmetic and copies ran while one was open for 0% -> 1% of each run, Pallas kernels for 0% -> 3%
where the time goes in v3:
time: 23.8 us; the launch traced here: 23.6 us
  starting transfers between devices  9.13 us (38%)
  waiting for transfers between devices  8.81 us (37%)
  Pallas kernels  3.46 us (15%)
  between operations  1.39 us (6%)
  other arithmetic  0.73 us (3%)
    ppermute x6, starting transfers between devices, swap(): got.append(lax.ppermute(blocks[step], ('dp', 'rollout'), pairs))  9.06 us
    ppermute x6, waiting for transfers between devices, swap(): got.append(lax.ppermute(blocks[step], ('dp', 'rollout'), pairs))  8.46 us
    pallas_call x1, Pallas kernels, product_blocks(): pl.pallas_call(functools.partial(product_kernel, inner, outer, chunks), o...  2.44 us
    pallas_call x1, Pallas kernels, stored(): pl.pallas_call(store_kernel, out_shape=[jax.ShapeDtypeStruct(shape, jnp.f...  0.81 us
    select_n x1, other arithmetic, per_device(): jnp.where((bucket_owner == lax.axis_index('rollout'))[:, None, None], rou...  0.71 us
  transfers between devices with their start and end apart: 7, of which 7 were waited for; matrix products, arithmetic and copies ran while one was open for 1% of the time, Pallas kernels for 3%

profile of v3, /device:TPU:0, one launch (start us, length us, event | category | flops | bytes accessed | tf_op | source)
XLA Modules:
  0.0 23.6 jit_solution(5448483643045638595)
XLA Ops:
  0.6 0.0 copy-start.4
  0.6 0.0 copy-start.2
  0.7 0.0 copy-start
  0.7 0.0 copy-start.1
  0.7 2.4 %product.1 = (bf16[32,2048]{1,0:T(8,128)(2,1)S(1)}, bf16[32,2048]{1,0:T(8,128)(2,1)S(1)}, bf16[32,2048]{1,0:T(8,128)(2,1)S(1)}, bf16[32,2048]{1,0:T(8,128)(2,1)S(1)}) custom-call(bf16[768,128]{1,0:T(8,128)(2,1)} %bitcast.9, bf16[768,2048]{1,0:T(8,128)(2,1)} %bitcast.8), custom_call_target="tpu_custom_call" | custom-call | tf_op jit(solution)/shard_map/product/pallas_call | solution.py:59
  3.1 4.0 %collective-permute-start = (bf16[32,2048]{1,0:T(8,128)(2,1)S(1)}, bf16[32,2048]{1,0:T(8,128)(2,1)S(1)}, u32[]{:S(2)}, u32[]{:S(2)}) collective-permute-start(bf16[32,2048]{1,0:T(8,128)(2,1)S(1)} %get-tuple-element.18), channel_id=1, source_target_pairs={{0,6},{1,25},{2,4},{3,27},{4,2},{5,29},{6,0},{7,31},{8,14},{9,17},... | collective-permute-start | bytes 393224 | tf_op jit(solution)/shard_map/ppermute | solution.py:180
  7.1 0.5 %collective-permute-start.1 = (bf16[32,2048]{1,0:T(8,128)(2,1)S(1)}, bf16[32,2048]{1,0:T(8,128)(2,1)S(1)}, u32[]{:S(2)}, u32[]{:S(2)}) collective-permute-start(bf16[32,2048]{1,0:T(8,128)(2,1)S(1)} %get-tuple-element.19), channel_id=1, source_target_pairs={{0,2},{1,9},{2,0},{3,11},{4,6},{5,13},{6,4},{7,15},{8,10},{9,1},{1... | collective-permute-start | bytes 393224 | tf_op jit(solution)/shard_map/ppermute | solution.py:180
  7.6 0.1 collective-permute-start.2
  8.4 1.7 %collective-permute-done.refs_1_ = bf16[32,2048]{1,0:T(8,128)(2,1)S(1)} collective-permute-done((bf16[32,2048]{1,0:T(8,128)(2,1)S(1)}, bf16[32,2048]{1,0:T(8,128)(2,1)S(1)}, u32[]{:S(2)}, u32[]{:S(2)}) %collective-permute-start) | collective-permute-done | bytes 131104 | tf_op jit(solution)/shard_map/ppermute | solution.py:180
  10.0 2.0 %collective-permute-done.1.refs_2_ = bf16[32,2048]{1,0:T(8,128)(2,1)S(1)} collective-permute-done((bf16[32,2048]{1,0:T(8,128)(2,1)S(1)}, bf16[32,2048]{1,0:T(8,128)(2,1)S(1)}, u32[]{:S(2)}, u32[]{:S(2)}) %collective-permute-start.1) | collective-permute-done | bytes 131104 | tf_op jit(solution)/shard_map/ppermute | solution.py:180
  12.1 0.5 %collective-permute-done.2.refs_3_ = bf16[32,2048]{1,0:T(8,128)(2,1)S(1)} collective-permute-done((bf16[32,2048]{1,0:T(8,128)(2,1)S(1)}, bf16[32,2048]{1,0:T(8,128)(2,1)S(1)}, u32[]{:S(2)}, u32[]{:S(2)}) %collective-permute-start.2) | collective-permute-done | bytes 131104 | tf_op jit(solution)/shard_map/ppermute | solution.py:180
  12.6 0.1 middle.1
  12.7 3.7 %collective-permute-start.3 = (f32[8,2048]{1,0:T(8,128)S(1)}, f32[8,2048]{1,0:T(8,128)S(1)}, u32[]{:S(2)}, u32[]{:S(2)}) collective-permute-start(f32[8,2048]{1,0:T(8,128)S(1)} %get-tuple-element.22), channel_id=1, source_target_pairs={{0,24},{1,7},{2,26},{3,5},{4,28},{5,3},{6,30},{7,1},{8,16},{9,15},... | collective-permute-start | bytes 196616 | tf_op jit(solution)/shard_map/ppermute | solution.py:180
  16.4 0.0 collective-permute-start.4
  16.4 0.8 %collective-permute-start.5 = (f32[8,2048]{1,0:T(8,128)S(1)}, f32[8,2048]{1,0:T(8,128)S(1)}, u32[]{:S(2)}, u32[]{:S(2)}) collective-permute-start(f32[8,2048]{1,0:T(8,128)S(1)} %get-tuple-element.24), channel_id=1, source_target_pairs={{0,16},{1,5},{2,18},{3,7},{4,20},{5,1},{6,22},{7,3},{8,24},{9,13},... | collective-permute-start | bytes 196616 | tf_op jit(solution)/shard_map/ppermute | solution.py:180
  17.2 0.1 copy.12.refs_7_.step
  17.3 1.6 %collective-permute-done.3.refs_1_ = f32[8,2048]{1,0:T(8,128)S(1)} collective-permute-done((f32[8,2048]{1,0:T(8,128)S(1)}, f32[8,2048]{1,0:T(8,128)S(1)}, u32[]{:S(2)}, u32[]{:S(2)}) %collective-permute-start.3) | collective-permute-done | bytes 65568 | tf_op jit(solution)/shard_map/ppermute | solution.py:180
  18.8 1.8 %collective-permute-done.4.refs_2_ = f32[8,2048]{1,0:T(8,128)S(1)} collective-permute-done((f32[8,2048]{1,0:T(8,128)S(1)}, f32[8,2048]{1,0:T(8,128)S(1)}, u32[]{:S(2)}, u32[]{:S(2)}) %collective-permute-start.4) | collective-permute-done | bytes 65568 | tf_op jit(solution)/shard_map/ppermute | solution.py:180
  20.6 0.9 %collective-permute-done.5.refs_3_ = f32[8,2048]{1,0:T(8,128)S(1)} collective-permute-done((f32[8,2048]{1,0:T(8,128)S(1)}, f32[8,2048]{1,0:T(8,128)S(1)}, u32[]{:S(2)}, u32[]{:S(2)}) %collective-permute-start.5) | collective-permute-done | bytes 65568 | tf_op jit(solution)/shard_map/ppermute | solution.py:180
  21.6 0.1 publish.1
  21.7 0.1 collective-permute-start.6
  21.8 0.8 %store.1 = (f32[1,8,2048]{2,1,0:T(8,128)}, f32[1,8,2048]{2,1,0:T(8,128)}, f32[1,8,2048]{2,1,0:T(8,128)}) custom-call(f32[8,2048]{1,0:T(8,128)S(1)} %get-tuple-element.25.grad, f32[1,8,2048]{2,1,0:T(8,128)S(1)} %copy-done, f32[1,8,2048]{2,1,0:T(8,128)S(1)} %copy-done.1, f32[1,8,2048]{2,1,0:T(8,128)S(1)} %copy-done.2, f32[2,1,1]{2,1,0:T(1,128)S(1)} %copy.12.refs_7_.step), custom_call_target="tpu_custom_call" | custom-call | flops 1048576 | bytes 1048576 | tf_op jit(solution)/shard_map/store/pallas_call | solution.py:152
  22.6 0.4 %collective-permute-done.6 = bf16[1,8,2048]{2,1,0:T(8,128)(2,1)S(1)} collective-permute-done((bf16[1,8,2048]{2,1,0:T(8,128)(2,1)S(1)}, bf16[1,8,2048]{2,1,0:T(8,128)(2,1)S(1)}, u32[]{:S(2)}, u32[]{:S(2)}) %collective-permute-start.6) | collective-permute-done | bytes 32800 | tf_op jit(solution)/shard_map/ppermute | solution.py:199
  22.9 0.7 %broadcast_select_fusion = bf16[2,8,2048]{2,1,0:T(8,128)(2,1)} fusion(pred[2]{0:T(512)(128)(4,1)S(1)} %broadcast_compare_fusion, bf16[8,2048]{1,0:T(8,128)(2,1)S(1)} %bitcast.10, bf16[8,2048]{1,0:T(8,128)(2,1)S(1)} %bitcast.7), kind=kLoop, calls=%fused_computation | loop fusion | flops 32768 | bytes 131074 | tf_op jit(solution)/shard_map/jit(_where)/select_n | solution.py:200
  (8 shorter events, 0.0 us)
Async XLA Ops:
  0.6 16.5 %copy-start.4 = (f32[2]{0:T(128)S(1)}, f32[2]{0:T(128)}, u32[]{:S(2)}) copy-start(f32[2]{0:T(128)} %constant.10.clone) | copy-start | bytes 28
  0.6 20.9 %copy-start.2 = (f32[1,8,2048]{2,1,0:T(8,128)S(1)}, f32[1,8,2048]{2,1,0:T(8,128)}, u32[]{:S(2)}) copy-start(f32[1,8,2048]{2,1,0:T(8,128)} %master.1) | copy-start | bytes 196612
  0.7 20.9 %copy-start = (f32[1,8,2048]{2,1,0:T(8,128)S(1)}, f32[1,8,2048]{2,1,0:T(8,128)}, u32[]{:S(2)}) copy-start(f32[1,8,2048]{2,1,0:T(8,128)} %first.1) | copy-start | bytes 196612
  0.7 20.9 %copy-start.1 = (f32[1,8,2048]{2,1,0:T(8,128)S(1)}, f32[1,8,2048]{2,1,0:T(8,128)}, u32[]{:S(2)}) copy-start(f32[1,8,2048]{2,1,0:T(8,128)} %second.1) | copy-start | bytes 196612
  0.7 21.1 %copy-start.3 = (s32[2]{0:T(128)S(1)}, s32[2]{0:T(128)}, u32[]{:S(2)}) copy-start(s32[2]{0:T(128)} %param.14) | copy-start | bytes 28
  3.1 6.9 %collective-permute-start = (bf16[32,2048]{1,0:T(8,128)(2,1)S(1)}, bf16[32,2048]{1,0:T(8,128)(2,1)S(1)}, u32[]{:S(2)}, u32[]{:S(2)}) collective-permute-start(bf16[32,2048]{1,0:T(8,128)(2,1)S(1)} %get-tuple-element.18), channel_id=1, source_target_pairs={{0,6},{1,25},{2,4},{3,27},{4,2},{5,29},{6,0},{7,31},{8,14},{9,17},... | collective-permute-start | bytes 393224 | tf_op jit(solution)/shard_map/ppermute | solution.py:180
  7.1 5.0 %collective-permute-start.1 = (bf16[32,2048]{1,0:T(8,128)(2,1)S(1)}, bf16[32,2048]{1,0:T(8,128)(2,1)S(1)}, u32[]{:S(2)}, u32[]{:S(2)}) collective-permute-start(bf16[32,2048]{1,0:T(8,128)(2,1)S(1)} %get-tuple-element.19), channel_id=1, source_target_pairs={{0,2},{1,9},{2,0},{3,11},{4,6},{5,13},{6,4},{7,15},{8,10},{9,1},{1... | collective-permute-start | bytes 393224 | tf_op jit(solution)/shard_map/ppermute | solution.py:180
  7.6 5.0 %collective-permute-start.2 = (bf16[32,2048]{1,0:T(8,128)(2,1)S(1)}, bf16[32,2048]{1,0:T(8,128)(2,1)S(1)}, u32[]{:S(2)}, u32[]{:S(2)}) collective-permute-start(bf16[32,2048]{1,0:T(8,128)(2,1)S(1)} %get-tuple-element.20), channel_id=1, source_target_pairs={{0,4},{1,17},{2,6},{3,19},{4,0},{5,21},{6,2},{7,23},{8,12},{9,25},... | collective-permute-start | bytes 393224 | tf_op jit(solution)/shard_map/ppermute | solution.py:180
  12.7 6.1 %collective-permute-start.3 = (f32[8,2048]{1,0:T(8,128)S(1)}, f32[8,2048]{1,0:T(8,128)S(1)}, u32[]{:S(2)}, u32[]{:S(2)}) collective-permute-start(f32[8,2048]{1,0:T(8,128)S(1)} %get-tuple-element.22), channel_id=1, source_target_pairs={{0,24},{1,7},{2,26},{3,5},{4,28},{5,3},{6,30},{7,1},{8,16},{9,15},... | collective-permute-start | bytes 196616 | tf_op jit(solution)/shard_map/ppermute | solution.py:180
  16.4 4.3 %collective-permute-start.4 = (f32[8,2048]{1,0:T(8,128)S(1)}, f32[8,2048]{1,0:T(8,128)S(1)}, u32[]{:S(2)}, u32[]{:S(2)}) collective-permute-start(f32[8,2048]{1,0:T(8,128)S(1)} %get-tuple-element.23), channel_id=1, source_target_pairs={{0,8},{1,3},{2,10},{3,1},{4,12},{5,7},{6,14},{7,5},{8,0},{9,11},{1... | collective-permute-start | bytes 196616 | tf_op jit(solution)/shard_map/ppermute | solution.py:180
  16.4 5.2 %collective-permute-start.5 = (f32[8,2048]{1,0:T(8,128)S(1)}, f32[8,2048]{1,0:T(8,128)S(1)}, u32[]{:S(2)}, u32[]{:S(2)}) collective-permute-start(f32[8,2048]{1,0:T(8,128)S(1)} %get-tuple-element.24), channel_id=1, source_target_pairs={{0,16},{1,5},{2,18},{3,7},{4,20},{5,1},{6,22},{7,3},{8,24},{9,13},... | collective-permute-start | bytes 196616 | tf_op jit(solution)/shard_map/ppermute | solution.py:180
  21.7 1.3 %collective-permute-start.6 = (bf16[1,8,2048]{2,1,0:T(8,128)(2,1)S(1)}, bf16[1,8,2048]{2,1,0:T(8,128)(2,1)S(1)}, u32[]{:S(2)}, u32[]{:S(2)}) collective-permute-start(bf16[1,8,2048]{2,1,0:T(8,128)(2,1)S(1)} %get-tuple-element.29), channel_id=1, source_target_pairs={{0,1},{1,0},{2,3},{3,2},{4,5},{5,4},{6,7},{7,6},{8,9},{9,8},{10,11... | collective-permute-start | bytes 98312 | tf_op jit(solution)/shard_map/ppermute | solution.py:199

commit v4 on v3

--- a/solution.py
+++ b/solution.py
@@ -13,17 +13,21 @@
     return (lax.axis_index("rollout") % 2 == 1) if inner == outer else (lax.axis_index("rollout") < 0)
 
 
-def distance(step, count):
-    return 0 if step == 0 else (step + count - 3) % (count - 1) + 1
-
-
-def product_kernel(inner, outer, chunks, features_hbm, upstream_hbm, *refs):
+def plane_peer(mine, step, count):
+    return mine ^ (0 if step == 0 else (step + count - 3) % (count - 1) + 1)
+
+
+def line_peer(mine, step, count):
+    return (mine + step) & (count - 1)
+
+
+def product_kernel(inner, outer, cuts, features_hbm, upstream_hbm, *refs):
     blocks, (features, upstream, product, sems) = refs[:inner], refs[inner:]
-    depth = upstream.shape[0] // chunks
+    chunks = len(cuts) - 1
     rows = product.shape[0] // (inner * outer)
     copies = []
     for c in range(chunks):
-        part = pl.ds(c * depth, depth)
+        part = pl.ds(cuts[c], cuts[c + 1] - cuts[c])
         pair = (
             pltpu.make_async_copy(features_hbm.at[part], features.at[part], sems.at[c, 0]),
             pltpu.make_async_copy(upstream_hbm.at[part], upstream.at[part], sems.at[c, 1]),
@@ -36,7 +40,7 @@
     peer_step = jnp.where(turned, inner, 1)
     other_step = jnp.where(turned, 1, inner)
     for c in range(chunks):
-        part = slice(c * depth, (c + 1) * depth)
+        part = slice(cuts[c], cuts[c + 1])
         for copy in copies[c]:
             copy.wait()
         term = lax.dot_general(
@@ -44,7 +48,7 @@
         )
         product[...] = term if c == 0 else product[...] + term
     for d in range(inner):
-        peer = jnp.bitwise_xor(mine, distance(d, inner))
+        peer = jnp.where(turned, line_peer(mine, d, inner), plane_peer(mine, d, inner))
         for o in range(0, outer, 2):
             places = [((o + i) * other_step + peer * peer_step) * rows for i in range(2)]
             parts = [product[pl.ds(pl.multiple_of(at, rows), rows), :] for at in places]
@@ -54,10 +58,12 @@
 def product_blocks(features, upstream, inner, outer):
     tokens, rows = features.shape
     ff = upstream.shape[1]
-    chunks = 3 if tokens % 384 == 0 else 1
+    shares = [0, 1, 2, 3]
+    unit = tokens // shares[-1]
+    cuts = [share * unit for share in shares] if tokens % (16 * shares[-1]) == 0 else [0, tokens]
     block = pltpu.VMEM((rows // inner, ff), jnp.bfloat16)
     return pl.pallas_call(
-        functools.partial(product_kernel, inner, outer, chunks),
+        functools.partial(product_kernel, inner, outer, cuts),
         out_shape=[block] * inner,
         in_specs=[pl.BlockSpec(memory_space=pltpu.HBM)] * 2,
         out_specs=[VMEM_SPEC] * inner,
@@ -65,7 +71,7 @@
             pltpu.VMEM((tokens, rows), jnp.bfloat16),
             pltpu.VMEM((tokens, ff), jnp.bfloat16),
             pltpu.VMEM((rows, ff), jnp.float32),
-            pltpu.SemaphoreType.DMA((chunks, 2)),
+            pltpu.SemaphoreType.DMA((len(cuts) - 1, 2)),
         ],
         compiler_params=pltpu.CompilerParams(vmem_limit_bytes=24 * 2**20),
         name="product",
@@ -82,7 +88,7 @@
     turned = turned_here(inner, outer)
     mine = jnp.where(turned, lax.rem(lax.axis_index("dp"), inner), lax.axis_index("dp") // inner)
     for d in range(outer):
-        peer = jnp.bitwise_xor(mine, distance(d, outer))
+        peer = jnp.where(turned, plane_peer(mine, d, outer), line_peer(mine, d, outer))
         sent[d][...] = total[pl.ds(pl.multiple_of(peer * rows, rows), rows), :].astype(sent[d].dtype)
 
 
@@ -168,15 +174,19 @@
     return inner, n // inner
 
 
-def swap(blocks, strides, n, n_ro):
+def swap(blocks, level, inner, n, n_ro):
     count = len(blocks)
     got = [blocks[0]]
     for step in range(1, count):
         pairs = []
         for i in range(n):
             for r in range(n_ro):
-                turned = r % 2 if strides[0] != strides[1] else 0
-                pairs.append((i * n_ro + r, (i ^ (distance(step, count) * strides[turned])) * n_ro + r))
+                turned = r % 2 == 1 and inner * inner == n
+                line = turned if level == 1 else not turned
+                stride, rule = (inner, line_peer if level == 1 else line_peer) if line else (1, plane_peer)
+                mine = i // stride % count
+                to = i + (rule(mine, step, count) - mine) * stride
+                pairs.append((i * n_ro + r, to * n_ro + r))
         got.append(lax.ppermute(blocks[step], ("dp", "rollout"), pairs))
     return got
 
@@ -187,13 +197,12 @@
 
     def per_device(layer_inputs, cotangent, master, first_moment, second_moment, step_count, bucket_owner):
         inner, outer = split_of(n_dp)
-        strides = (1, inner) if inner == outer else (1, 1)
         blocks = product_blocks(layer_inputs[0], cotangent[0], inner, outer)
-        parts = middle_sums(swap(blocks, strides, n_dp, n_ro), inner, outer)
+        parts = middle_sums(swap(blocks, 1, inner, n_dp, n_ro), inner, outer)
         counts = (step_count + 1).astype(jnp.float32)
         corrections = 1.0 - jnp.power(jnp.array([0.9, 0.999], jnp.float32), counts)
         state = (first_moment, second_moment, master, corrections[:, None, None])
-        grad, rounded = to_publish(swap(parts, strides[::-1], n_dp, n_ro), state)
+        grad, rounded = to_publish(swap(parts, 2, inner, n_dp, n_ro), state)
         new_master, new_first, new_second = stored(grad, state)
         if n_ro == 2:
             other = lax.ppermute(rounded, "rollout", [(0, 1), (1, 0)])

time: 23.8 us -> 23.4 us (0.983)
  waiting for transfers between devices: 8.81 us -> 7.35 us
  starting transfers between devices: 9.13 us -> 10.2 us
    ppermute x6, waiting for transfers between devices: 8.46 us -> 7 us  [swap(): got.append(lax.ppermute(blocks[step], ('dp', 'rollout'), pairs))]
    ppermute x6, starting transfers between devices: 9.06 us -> 10.2 us  [swap(): got.append(lax.ppermute(blocks[step], ('dp', 'rollout'), pairs))]
where the time goes in v4:
time: 23.4 us; the launch traced here: 23.3 us
  starting transfers between devices  10.2 us (44%)
  waiting for transfers between devices  7.35 us (31%)
  Pallas kernels  3.46 us (15%)
  between operations  1.39 us (6%)
  other arithmetic  0.73 us (3%)
    ppermute x6, starting transfers between devices, swap(): got.append(lax.ppermute(blocks[step], ('dp', 'rollout'), pairs))  10.2 us
    ppermute x6, waiting for transfers between devices, swap(): got.append(lax.ppermute(blocks[step], ('dp', 'rollout'), pairs))  7 us
    pallas_call x1, Pallas kernels, product_blocks(): pl.pallas_call(functools.partial(product_kernel, inner, outer, cuts), out...  2.44 us
    pallas_call x1, Pallas kernels, stored(): pl.pallas_call(store_kernel, out_shape=[jax.ShapeDtypeStruct(shape, jnp.f...  0.81 us
    select_n x1, other arithmetic, per_device(): jnp.where((bucket_owner == lax.axis_index('rollout'))[:, None, None], rou...  0.71 us
  transfers between devices with their start and end apart: 7, of which 7 were waited for; matrix products, arithmetic and copies ran while one was open for 1% of the time, Pallas kernels for 3%

profile of v4, /device:TPU:0, one launch (start us, length us, event | category | flops | bytes accessed | tf_op | source)
XLA Modules:
  0.0 23.3 jit_solution(246123264123202787)
XLA Ops:
  0.6 0.0 copy-start.4
  0.6 0.0 copy-start.2
  0.7 0.0 copy-start
  0.7 2.4 %product.1 = (bf16[32,2048]{1,0:T(8,128)(2,1)S(1)}, bf16[32,2048]{1,0:T(8,128)(2,1)S(1)}, bf16[32,2048]{1,0:T(8,128)(2,1)S(1)}, bf16[32,2048]{1,0:T(8,128)(2,1)S(1)}) custom-call(bf16[768,128]{1,0:T(8,128)(2,1)} %bitcast.9, bf16[768,2048]{1,0:T(8,128)(2,1)} %bitcast.8), custom_call_target="tpu_custom_call" | custom-call | tf_op jit(solution)/shard_map/product/pallas_call | solution.py:65
  3.1 4.0 %collective-permute-start = (bf16[32,2048]{1,0:T(8,128)(2,1)S(1)}, bf16[32,2048]{1,0:T(8,128)(2,1)S(1)}, u32[]{:S(2)}, u32[]{:S(2)}) collective-permute-start(bf16[32,2048]{1,0:T(8,128)(2,1)S(1)} %get-tuple-element.18), channel_id=1, source_target_pairs={{0,6},{1,9},{2,4},{3,11},{4,2},{5,13},{6,0},{7,15},{8,14},{9,17},{... | collective-permute-start | bytes 393224 | tf_op jit(solution)/shard_map/ppermute | solution.py:190
  7.1 0.5 %collective-permute-start.1 = (bf16[32,2048]{1,0:T(8,128)(2,1)S(1)}, bf16[32,2048]{1,0:T(8,128)(2,1)S(1)}, u32[]{:S(2)}, u32[]{:S(2)}) collective-permute-start(bf16[32,2048]{1,0:T(8,128)(2,1)S(1)} %get-tuple-element.19), channel_id=1, source_target_pairs={{0,2},{1,17},{2,0},{3,19},{4,6},{5,21},{6,4},{7,23},{8,10},{9,25},... | collective-permute-start | bytes 393224 | tf_op jit(solution)/shard_map/ppermute | solution.py:190
  7.6 0.1 collective-permute-start.2
  8.4 1.7 %collective-permute-done.refs_1_ = bf16[32,2048]{1,0:T(8,128)(2,1)S(1)} collective-permute-done((bf16[32,2048]{1,0:T(8,128)(2,1)S(1)}, bf16[32,2048]{1,0:T(8,128)(2,1)S(1)}, u32[]{:S(2)}, u32[]{:S(2)}) %collective-permute-start) | collective-permute-done | bytes 131104 | tf_op jit(solution)/shard_map/ppermute | solution.py:190
  10.0 2.0 %collective-permute-done.1.refs_2_ = bf16[32,2048]{1,0:T(8,128)(2,1)S(1)} collective-permute-done((bf16[32,2048]{1,0:T(8,128)(2,1)S(1)}, bf16[32,2048]{1,0:T(8,128)(2,1)S(1)}, u32[]{:S(2)}, u32[]{:S(2)}) %collective-permute-start.1) | collective-permute-done | bytes 131104 | tf_op jit(solution)/shard_map/ppermute | solution.py:190
  12.1 0.5 %collective-permute-done.2.refs_3_ = bf16[32,2048]{1,0:T(8,128)(2,1)S(1)} collective-permute-done((bf16[32,2048]{1,0:T(8,128)(2,1)S(1)}, bf16[32,2048]{1,0:T(8,128)(2,1)S(1)}, u32[]{:S(2)}, u32[]{:S(2)}) %collective-permute-start.2) | collective-permute-done | bytes 131104 | tf_op jit(solution)/shard_map/ppermute | solution.py:190
  12.6 0.1 middle.1
  12.7 1.6 %collective-permute-start.3 = (f32[8,2048]{1,0:T(8,128)S(1)}, f32[8,2048]{1,0:T(8,128)S(1)}, u32[]{:S(2)}, u32[]{:S(2)}) collective-permute-start(f32[8,2048]{1,0:T(8,128)S(1)} %get-tuple-element.22), channel_id=1, source_target_pairs={{0,8},{1,7},{2,10},{3,5},{4,12},{5,3},{6,14},{7,1},{8,16},{9,15},{... | collective-permute-start | bytes 196616 | tf_op jit(solution)/shard_map/ppermute | solution.py:190
  14.3 2.6 %collective-permute-start.4 = (f32[8,2048]{1,0:T(8,128)S(1)}, f32[8,2048]{1,0:T(8,128)S(1)}, u32[]{:S(2)}, u32[]{:S(2)}) collective-permute-start(f32[8,2048]{1,0:T(8,128)S(1)} %get-tuple-element.23), channel_id=1, source_target_pairs={{0,16},{1,3},{2,18},{3,1},{4,20},{5,7},{6,22},{7,5},{8,24},{9,11},... | collective-permute-start | bytes 196616 | tf_op jit(solution)/shard_map/ppermute | solution.py:190
  16.9 1.3 %collective-permute-start.5 = (f32[8,2048]{1,0:T(8,128)S(1)}, f32[8,2048]{1,0:T(8,128)S(1)}, u32[]{:S(2)}, u32[]{:S(2)}) collective-permute-start(f32[8,2048]{1,0:T(8,128)S(1)} %get-tuple-element.24), channel_id=1, source_target_pairs={{0,24},{1,5},{2,26},{3,7},{4,28},{5,1},{6,30},{7,3},{8,0},{9,13},{... | collective-permute-start | bytes 196616 | tf_op jit(solution)/shard_map/ppermute | solution.py:190
  18.3 0.1 copy.12.refs_7_.step
  18.4 0.4 %collective-permute-done.3.refs_1_ = f32[8,2048]{1,0:T(8,128)S(1)} collective-permute-done((f32[8,2048]{1,0:T(8,128)S(1)}, f32[8,2048]{1,0:T(8,128)S(1)}, u32[]{:S(2)}, u32[]{:S(2)}) %collective-permute-start.3) | collective-permute-done | bytes 65568 | tf_op jit(solution)/shard_map/ppermute | solution.py:190
  18.8 0.7 %collective-permute-done.4.refs_2_ = f32[8,2048]{1,0:T(8,128)S(1)} collective-permute-done((f32[8,2048]{1,0:T(8,128)S(1)}, f32[8,2048]{1,0:T(8,128)S(1)}, u32[]{:S(2)}, u32[]{:S(2)}) %collective-permute-start.4) | collective-permute-done | bytes 65568 | tf_op jit(solution)/shard_map/ppermute | solution.py:190
  19.5 1.7 %collective-permute-done.5.refs_3_ = f32[8,2048]{1,0:T(8,128)S(1)} collective-permute-done((f32[8,2048]{1,0:T(8,128)S(1)}, f32[8,2048]{1,0:T(8,128)S(1)}, u32[]{:S(2)}, u32[]{:S(2)}) %collective-permute-start.5) | collective-permute-done | bytes 65568 | tf_op jit(solution)/shard_map/ppermute | solution.py:190
  21.2 0.0 copy-done
  21.2 0.1 publish.1
  21.3 0.1 collective-permute-start.6
  21.4 0.8 %store.1 = (f32[1,8,2048]{2,1,0:T(8,128)}, f32[1,8,2048]{2,1,0:T(8,128)}, f32[1,8,2048]{2,1,0:T(8,128)}) custom-call(f32[8,2048]{1,0:T(8,128)S(1)} %get-tuple-element.25.grad, f32[1,8,2048]{2,1,0:T(8,128)S(1)} %copy-done, f32[1,8,2048]{2,1,0:T(8,128)S(1)} %copy-done.1, f32[1,8,2048]{2,1,0:T(8,128)S(1)} %copy-done.2, f32[2,1,1]{2,1,0:T(1,128)S(1)} %copy.12.refs_7_.step), custom_call_target="tpu_custom_call" | custom-call | flops 1048576 | bytes 1048576 | tf_op jit(solution)/shard_map/store/pallas_call | solution.py:158
  22.2 0.4 %collective-permute-done.6 = bf16[1,8,2048]{2,1,0:T(8,128)(2,1)S(1)} collective-permute-done((bf16[1,8,2048]{2,1,0:T(8,128)(2,1)S(1)}, bf16[1,8,2048]{2,1,0:T(8,128)(2,1)S(1)}, u32[]{:S(2)}, u32[]{:S(2)}) %collective-permute-start.6) | collective-permute-done | bytes 32800 | tf_op jit(solution)/shard_map/ppermute | solution.py:208
  22.6 0.7 %broadcast_select_fusion = bf16[2,8,2048]{2,1,0:T(8,128)(2,1)} fusion(pred[2]{0:T(512)(128)(4,1)S(1)} %broadcast_compare_fusion, bf16[8,2048]{1,0:T(8,128)(2,1)S(1)} %bitcast.10, bf16[8,2048]{1,0:T(8,128)(2,1)S(1)} %bitcast.7), kind=kLoop, calls=%fused_computation | loop fusion | flops 32768 | bytes 131074 | tf_op jit(solution)/shard_map/jit(_where)/select_n | solution.py:209
  (8 shorter events, 0.0 us)
Async XLA Ops:
  0.6 17.6 %copy-start.4 = (f32[2]{0:T(128)S(1)}, f32[2]{0:T(128)}, u32[]{:S(2)}) copy-start(f32[2]{0:T(128)} %constant.10.clone) | copy-start | bytes 28
  0.6 20.5 %copy-start.2 = (f32[1,8,2048]{2,1,0:T(8,128)S(1)}, f32[1,8,2048]{2,1,0:T(8,128)}, u32[]{:S(2)}) copy-start(f32[1,8,2048]{2,1,0:T(8,128)} %master.1) | copy-start | bytes 196612
  0.7 20.5 %copy-start = (f32[1,8,2048]{2,1,0:T(8,128)S(1)}, f32[1,8,2048]{2,1,0:T(8,128)}, u32[]{:S(2)}) copy-start(f32[1,8,2048]{2,1,0:T(8,128)} %first.1) | copy-start | bytes 196612
  0.7 20.5 %copy-start.1 = (f32[1,8,2048]{2,1,0:T(8,128)S(1)}, f32[1,8,2048]{2,1,0:T(8,128)}, u32[]{:S(2)}) copy-start(f32[1,8,2048]{2,1,0:T(8,128)} %second.1) | copy-start | bytes 196612
  0.7 20.7 %copy-start.3 = (s32[2]{0:T(128)S(1)}, s32[2]{0:T(128)}, u32[]{:S(2)}) copy-start(s32[2]{0:T(128)} %param.14) | copy-start | bytes 28
  3.1 6.9 %collective-permute-start = (bf16[32,2048]{1,0:T(8,128)(2,1)S(1)}, bf16[32,2048]{1,0:T(8,128)(2,1)S(1)}, u32[]{:S(2)}, u32[]{:S(2)}) collective-permute-start(bf16[32,2048]{1,0:T(8,128)(2,1)S(1)} %get-tuple-element.18), channel_id=1, source_target_pairs={{0,6},{1,9},{2,4},{3,11},{4,2},{5,13},{6,0},{7,15},{8,14},{9,17},{... | collective-permute-start | bytes 393224 | tf_op jit(solution)/shard_map/ppermute | solution.py:190
  7.1 5.0 %collective-permute-start.1 = (bf16[32,2048]{1,0:T(8,128)(2,1)S(1)}, bf16[32,2048]{1,0:T(8,128)(2,1)S(1)}, u32[]{:S(2)}, u32[]{:S(2)}) collective-permute-start(bf16[32,2048]{1,0:T(8,128)(2,1)S(1)} %get-tuple-element.19), channel_id=1, source_target_pairs={{0,2},{1,17},{2,0},{3,19},{4,6},{5,21},{6,4},{7,23},{8,10},{9,25},... | collective-permute-start | bytes 393224 | tf_op jit(solution)/shard_map/ppermute | solution.py:190
  7.6 5.0 %collective-permute-start.2 = (bf16[32,2048]{1,0:T(8,128)(2,1)S(1)}, bf16[32,2048]{1,0:T(8,128)(2,1)S(1)}, u32[]{:S(2)}, u32[]{:S(2)}) collective-permute-start(bf16[32,2048]{1,0:T(8,128)(2,1)S(1)} %get-tuple-element.20), channel_id=1, source_target_pairs={{0,4},{1,25},{2,6},{3,27},{4,0},{5,29},{6,2},{7,31},{8,12},{9,1},{... | collective-permute-start | bytes 393224 | tf_op jit(solution)/shard_map/ppermute | solution.py:190
  12.7 6.1 %collective-permute-start.3 = (f32[8,2048]{1,0:T(8,128)S(1)}, f32[8,2048]{1,0:T(8,128)S(1)}, u32[]{:S(2)}, u32[]{:S(2)}) collective-permute-start(f32[8,2048]{1,0:T(8,128)S(1)} %get-tuple-element.22), channel_id=1, source_target_pairs={{0,8},{1,7},{2,10},{3,5},{4,12},{5,3},{6,14},{7,1},{8,16},{9,15},{... | collective-permute-start | bytes 196616 | tf_op jit(solution)/shard_map/ppermute | solution.py:190
  14.3 5.2 %collective-permute-start.4 = (f32[8,2048]{1,0:T(8,128)S(1)}, f32[8,2048]{1,0:T(8,128)S(1)}, u32[]{:S(2)}, u32[]{:S(2)}) collective-permute-start(f32[8,2048]{1,0:T(8,128)S(1)} %get-tuple-element.23), channel_id=1, source_target_pairs={{0,16},{1,3},{2,18},{3,1},{4,20},{5,7},{6,22},{7,5},{8,24},{9,11},... | collective-permute-start | bytes 196616 | tf_op jit(solution)/shard_map/ppermute | solution.py:190
  16.9 4.3 %collective-permute-start.5 = (f32[8,2048]{1,0:T(8,128)S(1)}, f32[8,2048]{1,0:T(8,128)S(1)}, u32[]{:S(2)}, u32[]{:S(2)}) collective-permute-start(f32[8,2048]{1,0:T(8,128)S(1)} %get-tuple-element.24), channel_id=1, source_target_pairs={{0,24},{1,5},{2,26},{3,7},{4,28},{5,1},{6,30},{7,3},{8,0},{9,13},{... | collective-permute-start | bytes 196616 | tf_op jit(solution)/shard_map/ppermute | solution.py:190
  21.3 1.3 %collective-permute-start.6 = (bf16[1,8,2048]{2,1,0:T(8,128)(2,1)S(1)}, bf16[1,8,2048]{2,1,0:T(8,128)(2,1)S(1)}, u32[]{:S(2)}, u32[]{:S(2)}) collective-permute-start(bf16[1,8,2048]{2,1,0:T(8,128)(2,1)S(1)} %get-tuple-element.29), channel_id=1, source_target_pairs={{0,1},{1,0},{2,3},{3,2},{4,5},{5,4},{6,7},{7,6},{8,9},{9,8},{10,11... | collective-permute-start | bytes 98312 | tf_op jit(solution)/shard_map/ppermute | solution.py:208

commit v5 on v4

--- a/solution.py
+++ b/solution.py
@@ -18,7 +18,11 @@
 
 
 def line_peer(mine, step, count):
-    return (mine + step) & (count - 1)
+    if count != 4:
+        return (mine + step) & (count - 1)
+    place = (mine & 1) * 2 + (mine >> 1)
+    to = (place + (0, 1, 3, 2)[step]) & 3
+    return (to & 1) * 2 + (to >> 1)
 
 
 def product_kernel(inner, outer, cuts, features_hbm, upstream_hbm, *refs):
@@ -78,8 +82,8 @@
     )(*(pltpu.with_memory_space_constraint(x, pltpu.HBM) for x in (features, upstream)))
 
 
-def middle_kernel(inner, outer, *refs):
-    got, sent, total = refs[:inner], refs[inner : inner + outer], refs[-1]
+def middle_kernel(inner, outer, packs, *refs):
+    got, state, sent, total = refs[:inner], refs[inner : inner + packs], refs[inner + packs : -1], refs[-1]
     acc = got[0][...].astype(jnp.float32)
     for g in got[1:]:
         acc = acc + g[...].astype(jnp.float32)
@@ -89,22 +93,27 @@
     mine = jnp.where(turned, lax.rem(lax.axis_index("dp"), inner), lax.axis_index("dp") // inner)
     for d in range(outer):
         peer = jnp.where(turned, plane_peer(mine, d, outer), line_peer(mine, d, outer))
-        sent[d][...] = total[pl.ds(pl.multiple_of(peer * rows, rows), rows), :].astype(sent[d].dtype)
-
-
-def middle_sums(got, inner, outer):
+        sent[d][:, : total.shape[1]] = total[pl.ds(pl.multiple_of(peer * rows, rows), rows), :].astype(sent[d].dtype)
+    if packs:
+        cross, ff = sent[outer - 1], total.shape[1]
+        for k in range(2):
+            cross[:, ff + k * 128 : ff + (k + 1) * 128] = jnp.broadcast_to(state[0][k], (rows, 128))
+
+
+def middle_sums(got, inner, outer, state=()):
     rows, ff = got[0].shape
     part = pltpu.VMEM((rows // outer, ff), jnp.float32)
-    got = [pltpu.with_memory_space_constraint(g, pltpu.VMEM) for g in got]
-    return pl.pallas_call(
-        functools.partial(middle_kernel, inner, outer),
-        out_shape=[part] * outer,
-        in_specs=[VMEM_SPEC] * inner,
+    packed = [pltpu.VMEM((rows // outer, ff + 256), jnp.float32)] if state else []
+    args = held_in_vmem((*got, *state))
+    return pl.pallas_call(
+        functools.partial(middle_kernel, inner, outer, len(state)),
+        out_shape=[part] * (outer - len(packed)) + packed,
+        in_specs=[VMEM_SPEC] * len(args),
         out_specs=[VMEM_SPEC] * outer,
         scratch_shapes=[pltpu.VMEM((rows, ff), jnp.float32)],
         compiler_params=pltpu.CompilerParams(vmem_limit_bytes=8 * 2**20),
         name="middle",
-    )(*got)
+    )(*args)
 
 
 def stepped(grad, first, second, master, step):
@@ -167,6 +176,86 @@
     )(*args)
 
 
+def pack_kernel(first, second, master, anchor, out):
+    for k, ref in enumerate((first, second, master)):
+        out[k] = ref[0]
+
+
+def packed_state(state, anchor):
+    return pl.pallas_call(
+        pack_kernel,
+        out_shape=pltpu.VMEM((3, *state[0].shape[1:]), jnp.float32),
+        in_specs=[VMEM_SPEC] * 4,
+        out_specs=VMEM_SPEC,
+        compiler_params=pltpu.CompilerParams(vmem_limit_bytes=4 * 2**20),
+        name="pack",
+    )(*held_in_vmem((*state[:3], anchor)))
+
+
+def partial_kernel(*refs):
+    acc = refs[0][...]
+    for ref in refs[1:-1]:
+        acc = acc + ref[...]
+    refs[-1][...] = acc
+
+
+def partial_sum(parts):
+    return pl.pallas_call(
+        partial_kernel,
+        out_shape=pltpu.VMEM(parts[0].shape, jnp.float32),
+        in_specs=[VMEM_SPEC] * len(parts),
+        out_specs=VMEM_SPEC,
+        compiler_params=pltpu.CompilerParams(vmem_limit_bytes=4 * 2**20),
+        name="partial",
+    )(*held_in_vmem(parts))
+
+
+def finish_kernel(
+    part, last, far_part, far_last, first, second, master, step, far, mask, *refs
+):
+    outs, published, (held, rounded, sems) = refs[:3], refs[3], refs[4:]
+    copies = []
+    ours = stepped(part[...] + last[:, : part.shape[1]], first, second, master, step)
+    ff = part.shape[1]
+    steps = [far_last[:, ff + k * 128 : ff + k * 128 + 1] for k in range(2)]
+    theirs = stepped(far_part[...] + far_last[:, :ff], far.at[0:1], far.at[1:2], far.at[2:3], steps)[0]
+    here = mask[...] > 0
+    rounded[0] = jnp.where(here, ours[0], theirs).astype(jnp.bfloat16)
+    rounded[1] = jnp.where(here, theirs, ours[0]).astype(jnp.bfloat16)
+    copies.append(pltpu.make_async_copy(rounded, published, sems.at[3]))
+    copies[0].start()
+    for k, value in enumerate(ours):
+        held[k] = value
+        copy = pltpu.make_async_copy(held.at[k], outs[k].at[0], sems.at[k])
+        copy.start()
+        copies.append(copy)
+    for copy in copies:
+        copy.wait()
+
+
+def finished(part, last, far_part, far_last, state, far, mask):
+    shape = state[0].shape
+    args = held_in_vmem((part, last, far_part, far_last, *state, far, mask))
+    return pl.pallas_call(
+        finish_kernel,
+        out_shape=[jax.ShapeDtypeStruct(shape, jnp.float32)] * 3
+        + [jax.ShapeDtypeStruct((2, *shape[1:]), jnp.bfloat16)],
+        in_specs=[VMEM_SPEC] * len(args),
+        out_specs=[pl.BlockSpec(memory_space=pltpu.HBM)] * 4,
+        scratch_shapes=[
+            pltpu.VMEM((3, *shape[1:]), jnp.float32),
+            pltpu.VMEM((2, *shape[1:]), jnp.bfloat16),
+            pltpu.SemaphoreType.DMA((4,)),
+        ],
+        compiler_params=pltpu.CompilerParams(vmem_limit_bytes=8 * 2**20),
+        name="finish",
+    )(*args)
+
+
+def over_cores(x):
+    return lax.ppermute(x, "rollout", [(0, 1), (1, 0)])
+
+
 def split_of(n):
     inner = 1
     while inner * inner < n:
@@ -174,21 +263,22 @@
     return inner, n // inner
 
 
+def exchange(block, step, count, level, inner, n, n_ro, cross=0):
+    pairs = []
+    for i in range(n):
+        for r in range(n_ro):
+            turned = r % 2 == 1 and inner * inner == n
+            line = turned if level == 1 else not turned
+            stride, rule = (inner, line_peer) if line else (1, plane_peer)
+            mine = i // stride % count
+            to = i + (rule(mine, step, count) - mine) * stride
+            pairs.append((i * n_ro + r, to * n_ro + (r ^ cross)))
+    return lax.ppermute(block, ("dp", "rollout"), pairs)
+
+
 def swap(blocks, level, inner, n, n_ro):
     count = len(blocks)
-    got = [blocks[0]]
-    for step in range(1, count):
-        pairs = []
-        for i in range(n):
-            for r in range(n_ro):
-                turned = r % 2 == 1 and inner * inner == n
-                line = turned if level == 1 else not turned
-                stride, rule = (inner, line_peer if level == 1 else line_peer) if line else (1, plane_peer)
-                mine = i // stride % count
-                to = i + (rule(mine, step, count) - mine) * stride
-                pairs.append((i * n_ro + r, to * n_ro + r))
-        got.append(lax.ppermute(blocks[step], ("dp", "rollout"), pairs))
-    return got
+    return [blocks[0]] + [exchange(blocks[k], k, count, level, inner, n, n_ro) for k in range(1, count)]
 
 
 def solution(mesh):
@@ -198,19 +288,22 @@
     def per_device(layer_inputs, cotangent, master, first_moment, second_moment, step_count, bucket_owner):
         inner, outer = split_of(n_dp)
         blocks = product_blocks(layer_inputs[0], cotangent[0], inner, outer)
-        parts = middle_sums(swap(blocks, 1, inner, n_dp, n_ro), inner, outer)
+        got = swap(blocks, 1, inner, n_dp, n_ro)
         counts = (step_count + 1).astype(jnp.float32)
         corrections = 1.0 - jnp.power(jnp.array([0.9, 0.999], jnp.float32), counts)
         state = (first_moment, second_moment, master, corrections[:, None, None])
-        grad, rounded = to_publish(swap(parts, 2, inner, n_dp, n_ro), state)
-        new_master, new_first, new_second = stored(grad, state)
-        if n_ro == 2:
-            other = lax.ppermute(rounded, "rollout", [(0, 1), (1, 0)])
-            published = jnp.where((bucket_owner == lax.axis_index("rollout"))[:, None, None], rounded, other)
-        else:
+        if n_ro != 2:
+            parts = middle_sums(got, inner, outer)
+            grad, rounded = to_publish(swap(parts, 2, inner, n_dp, n_ro), state)
             every_group = lax.all_gather(rounded, "rollout", axis=0, tiled=True)
-            published = jnp.take(every_group, bucket_owner, axis=0)
-        return new_master, new_first, new_second, published
+            return (*stored(grad, state), jnp.take(every_group, bucket_owner, axis=0))
+        parts = middle_sums(got, inner, outer, state[3:])
+        mine = swap(parts, 2, inner, n_dp, n_ro)
+        far_last = exchange(parts[-1], outer - 1, outer, 2, inner, n_dp, n_ro, cross=1)
+        far = over_cores(packed_state(state, blocks[0]))
+        part = partial_sum(mine[:-1])
+        mask = jnp.full((1, 1), bucket_owner[0] == lax.axis_index("rollout"), jnp.float32)
+        return tuple(finished(part, mine[-1], over_cores(part), far_last, state, far, mask))
 
     s = P("rollout", "dp", None)
     return jax.shard_map(

time: 23.4 us -> 22.9 us (0.979)
  waiting for transfers between devices: 7.35 us -> 8.43 us
  starting transfers between devices: 10.2 us -> 9.3 us
  other arithmetic: 0.73 us -> 0.02 us
    ppermute x7 -> x9, waiting for transfers between devices: 7.35 us -> 8.43 us  [the longest x7 7.85 us: exchange(): return lax.ppermute(block, ('dp', 'rollout'), pairs)]
    ppermute x7 -> x9, starting transfers between devices: 10.2 us -> 9.3 us  [the longest x7 8.8 us: exchange(): return lax.ppermute(block, ('dp', 'rollout'), pairs)]
    select_n x1 -> x0, other arithmetic: 0.71 us -> none  [per_device(): jnp.where((bucket_owner == lax.axis_index('rollout'))[:, None, None], rou...]
    pallas_call x3 -> x4, Pallas kernels: 1.02 us -> 1 us  [the longest x1 0.88 us: finished(): pl.pallas_call(finish_kernel, out_shape=[jax.ShapeDtypeStruct(shape, jnp....]
  transfers between devices with their start and end apart: 7 -> 9, of which waited for: 7 -> 7; matrix products, arithmetic and copies ran while one was open for 1% -> 0% of each run, Pallas kernels for 3% -> 1%
where the time goes in v5:
time: 22.9 us; the launch traced here: 22.7 us
  starting transfers between devices  9.3 us (41%)
  waiting for transfers between devices  8.43 us (37%)
  Pallas kernels  3.43 us (15%)
  between operations  1.43 us (6%)
    ppermute x7, starting transfers between devices, exchange(): return lax.ppermute(block, ('dp', 'rollout'), pairs)  8.8 us
    ppermute x7, waiting for transfers between devices, exchange(): return lax.ppermute(block, ('dp', 'rollout'), pairs)  7.85 us
    pallas_call x1, Pallas kernels, product_blocks(): pl.pallas_call(functools.partial(product_kernel, inner, outer, cuts), out...  2.43 us
    pallas_call x1, Pallas kernels, finished(): pl.pallas_call(finish_kernel, out_shape=[jax.ShapeDtypeStruct(shape, jnp....  0.88 us
    ppermute x2, waiting for transfers between devices, over_cores(): return lax.ppermute(x, 'rollout', [(0, 1), (1, 0)])  0.58 us
    ppermute x2, starting transfers between devices, over_cores(): return lax.ppermute(x, 'rollout', [(0, 1), (1, 0)])  0.5 us
  transfers between devices with their start and end apart: 9, of which 7 were waited for; matrix products, arithmetic and copies ran while one was open for 0% of the time, Pallas kernels for 1%

profile of v5, /device:TPU:0, one launch (start us, length us, event | category | flops | bytes accessed | tf_op | source)
XLA Modules:
  0.0 22.7 jit_solution(1930380759745882726)
XLA Ops:
  0.6 0.0 copy-start.4
  0.7 2.4 %product.1 = (bf16[32,2048]{1,0:T(8,128)(2,1)S(1)}, bf16[32,2048]{1,0:T(8,128)(2,1)S(1)}, bf16[32,2048]{1,0:T(8,128)(2,1)S(1)}, bf16[32,2048]{1,0:T(8,128)(2,1)S(1)}) custom-call(bf16[768,128]{1,0:T(8,128)(2,1)} %bitcast.9, bf16[768,2048]{1,0:T(8,128)(2,1)} %bitcast.8), custom_call_target="tpu_custom_call" | custom-call | tf_op jit(solution)/shard_map/product/pallas_call | solution.py:69
  3.1 3.9 %collective-permute-start = (bf16[32,2048]{1,0:T(8,128)(2,1)S(1)}, bf16[32,2048]{1,0:T(8,128)(2,1)S(1)}, u32[]{:S(2)}, u32[]{:S(2)}) collective-permute-start(bf16[32,2048]{1,0:T(8,128)(2,1)S(1)} %get-tuple-element.13), channel_id=1, source_target_pairs={{0,6},{1,17},{2,4},{3,19},{4,2},{5,21},{6,0},{7,23},{8,14},{9,25},... | collective-permute-start | bytes 393224 | tf_op jit(solution)/shard_map/ppermute | solution.py:276
  7.1 0.5 %collective-permute-start.1 = (bf16[32,2048]{1,0:T(8,128)(2,1)S(1)}, bf16[32,2048]{1,0:T(8,128)(2,1)S(1)}, u32[]{:S(2)}, u32[]{:S(2)}) collective-permute-start(bf16[32,2048]{1,0:T(8,128)(2,1)S(1)} %get-tuple-element.14), channel_id=1, source_target_pairs={{0,2},{1,25},{2,0},{3,27},{4,6},{5,29},{6,4},{7,31},{8,10},{9,17},... | collective-permute-start | bytes 393224 | tf_op jit(solution)/shard_map/ppermute | solution.py:276
  7.6 0.1 collective-permute-start.2
  7.7 0.0 copy-done
  7.7 0.4 %collective-permute-start.8 = (f32[3,8,2048]{2,1,0:T(8,128)S(1)}, f32[3,8,2048]{2,1,0:T(8,128)S(1)}, u32[]{:S(2)}, u32[]{:S(2)}) collective-permute-start(f32[3,8,2048]{2,1,0:T(8,128)S(1)} %pack.1), channel_id=1, source_target_pairs={{0,1},{1,0},{2,3},{3,2},{4,5},{5,4},{6,7},{7,6},{8,9},{9,8},{10,11... | collective-permute-start | bytes 589832 | tf_op jit(solution)/shard_map/ppermute | solution.py:256
  8.8 0.1 copy.12.refs_4_.step
  8.9 1.1 %collective-permute-done.refs_1_ = bf16[32,2048]{1,0:T(8,128)(2,1)S(1)} collective-permute-done((bf16[32,2048]{1,0:T(8,128)(2,1)S(1)}, bf16[32,2048]{1,0:T(8,128)(2,1)S(1)}, u32[]{:S(2)}, u32[]{:S(2)}) %collective-permute-start) | collective-permute-done | bytes 131104 | tf_op jit(solution)/shard_map/ppermute | solution.py:276
  10.0 2.0 %collective-permute-done.1.refs_2_ = bf16[32,2048]{1,0:T(8,128)(2,1)S(1)} collective-permute-done((bf16[32,2048]{1,0:T(8,128)(2,1)S(1)}, bf16[32,2048]{1,0:T(8,128)(2,1)S(1)}, u32[]{:S(2)}, u32[]{:S(2)}) %collective-permute-start.1) | collective-permute-done | bytes 131104 | tf_op jit(solution)/shard_map/ppermute | solution.py:276
  12.0 0.5 %collective-permute-done.2.refs_3_ = bf16[32,2048]{1,0:T(8,128)(2,1)S(1)} collective-permute-done((bf16[32,2048]{1,0:T(8,128)(2,1)S(1)}, bf16[32,2048]{1,0:T(8,128)(2,1)S(1)}, u32[]{:S(2)}, u32[]{:S(2)}) %collective-permute-start.2) | collective-permute-done | bytes 131104 | tf_op jit(solution)/shard_map/ppermute | solution.py:276
  12.6 0.1 middle.1
  12.7 2.6 %collective-permute-start.3 = (f32[8,2048]{1,0:T(8,128)S(1)}, f32[8,2048]{1,0:T(8,128)S(1)}, u32[]{:S(2)}, u32[]{:S(2)}) collective-permute-start(f32[8,2048]{1,0:T(8,128)S(1)} %get-tuple-element.17), channel_id=1, source_target_pairs={{0,16},{1,7},{2,18},{3,5},{4,20},{5,3},{6,22},{7,1},{8,24},{9,15},... | collective-permute-start | bytes 196616 | tf_op jit(solution)/shard_map/ppermute | solution.py:276
  15.3 1.2 %collective-permute-start.4 = (f32[8,2048]{1,0:T(8,128)S(1)}, f32[8,2048]{1,0:T(8,128)S(1)}, u32[]{:S(2)}, u32[]{:S(2)}) collective-permute-start(f32[8,2048]{1,0:T(8,128)S(1)} %get-tuple-element.18), channel_id=1, source_target_pairs={{0,24},{1,3},{2,26},{3,1},{4,28},{5,7},{6,30},{7,5},{8,16},{9,11},... | collective-permute-start | bytes 196616 | tf_op jit(solution)/shard_map/ppermute | solution.py:276
  16.5 0.3 %collective-permute-start.5 = (f32[8,2304]{1,0:T(8,128)S(1)}, f32[8,2304]{1,0:T(8,128)S(1)}, u32[]{:S(2)}, u32[]{:S(2)}) collective-permute-start(f32[8,2304]{1,0:T(8,128)S(1)} %get-tuple-element.19), channel_id=1, source_target_pairs={{0,8},{1,5},{2,10},{3,7},{4,12},{5,1},{6,14},{7,3},{8,0},{9,13},{1... | collective-permute-start | bytes 221192 | tf_op jit(solution)/shard_map/ppermute | solution.py:276
  16.9 0.0 collective-permute-start.7
  16.9 1.9 %collective-permute-done.3.refs_1_ = f32[8,2048]{1,0:T(8,128)S(1)} collective-permute-done((f32[8,2048]{1,0:T(8,128)S(1)}, f32[8,2048]{1,0:T(8,128)S(1)}, u32[]{:S(2)}, u32[]{:S(2)}) %collective-permute-start.3) | collective-permute-done | bytes 65568 | tf_op jit(solution)/shard_map/ppermute | solution.py:276
  18.8 1.7 %collective-permute-done.4.refs_2_ = f32[8,2048]{1,0:T(8,128)S(1)} collective-permute-done((f32[8,2048]{1,0:T(8,128)S(1)}, f32[8,2048]{1,0:T(8,128)S(1)}, u32[]{:S(2)}, u32[]{:S(2)}) %collective-permute-start.4) | collective-permute-done | bytes 65568 | tf_op jit(solution)/shard_map/ppermute | solution.py:276
  20.5 0.1 collective-permute-start.6
  20.7 0.0 collective-permute-done.8.far
  20.7 0.6 %collective-permute-done.5.last = f32[8,2304]{1,0:T(8,128)S(1)} collective-permute-done((f32[8,2304]{1,0:T(8,128)S(1)}, f32[8,2304]{1,0:T(8,128)S(1)}, u32[]{:S(2)}, u32[]{:S(2)}) %collective-permute-start.5) | collective-permute-done | bytes 73760 | tf_op jit(solution)/shard_map/ppermute | solution.py:276
  21.3 0.0 collective-permute-done.7.far_last
  21.3 0.6 %collective-permute-done.6.far_part = f32[8,2048]{1,0:T(8,128)S(1)} collective-permute-done((f32[8,2048]{1,0:T(8,128)S(1)}, f32[8,2048]{1,0:T(8,128)S(1)}, u32[]{:S(2)}, u32[]{:S(2)}) %collective-permute-start.6) | collective-permute-done | bytes 65568 | tf_op jit(solution)/shard_map/ppermute | solution.py:256
  21.8 0.9 %finish.1 = (f32[1,8,2048]{2,1,0:T(8,128)}, f32[1,8,2048]{2,1,0:T(8,128)}, f32[1,8,2048]{2,1,0:T(8,128)}, bf16[2,8,2048]{2,1,0:T(8,128)(2,1)}) custom-call(f32[8,2048]{1,0:T(8,128)S(1)} %partial.1.part, f32[8,2304]{1,0:T(8,128)S(1)} %collective-permute-done.5.last, f32[8,2048]{1,0:T(8,128)S(1)} %collective-permute-done.6.far_part, ...), custom_call_target="tpu_custom_call" | custom-call | tf_op jit(solution)/shard_map/finish/pallas_call | solution.py:239
  (11 shorter events, 0.1 us)
Async XLA Ops:
  0.6 8.2 %copy-start.4 = (f32[2]{0:T(128)S(1)}, f32[2]{0:T(128)}, u32[]{:S(2)}) copy-start(f32[2]{0:T(128)} %constant.10.clone) | copy-start | bytes 28
  0.6 7.1 %copy-start.2 = (f32[1,8,2048]{2,1,0:T(8,128)S(1)}, f32[1,8,2048]{2,1,0:T(8,128)}, u32[]{:S(2)}) copy-start(f32[1,8,2048]{2,1,0:T(8,128)} %master.3) | copy-start | bytes 196612
  0.7 7.0 %copy-start = (f32[1,8,2048]{2,1,0:T(8,128)S(1)}, f32[1,8,2048]{2,1,0:T(8,128)}, u32[]{:S(2)}) copy-start(f32[1,8,2048]{2,1,0:T(8,128)} %first.3) | copy-start | bytes 196612
  0.7 7.0 %copy-start.1 = (f32[1,8,2048]{2,1,0:T(8,128)S(1)}, f32[1,8,2048]{2,1,0:T(8,128)}, u32[]{:S(2)}) copy-start(f32[1,8,2048]{2,1,0:T(8,128)} %second.3) | copy-start | bytes 196612
  0.7 19.9 %copy-start.3 = (s32[2]{0:T(128)S(1)}, s32[2]{0:T(128)}, u32[]{:S(2)}) copy-start(s32[2]{0:T(128)} %param.14) | copy-start | bytes 28
  3.1 6.9 %collective-permute-start = (bf16[32,2048]{1,0:T(8,128)(2,1)S(1)}, bf16[32,2048]{1,0:T(8,128)(2,1)S(1)}, u32[]{:S(2)}, u32[]{:S(2)}) collective-permute-start(bf16[32,2048]{1,0:T(8,128)(2,1)S(1)} %get-tuple-element.13), channel_id=1, source_target_pairs={{0,6},{1,17},{2,4},{3,19},{4,2},{5,21},{6,0},{7,23},{8,14},{9,25},... | collective-permute-start | bytes 393224 | tf_op jit(solution)/shard_map/ppermute | solution.py:276
  7.1 5.0 %collective-permute-start.1 = (bf16[32,2048]{1,0:T(8,128)(2,1)S(1)}, bf16[32,2048]{1,0:T(8,128)(2,1)S(1)}, u32[]{:S(2)}, u32[]{:S(2)}) collective-permute-start(bf16[32,2048]{1,0:T(8,128)(2,1)S(1)} %get-tuple-element.14), channel_id=1, source_target_pairs={{0,2},{1,25},{2,0},{3,27},{4,6},{5,29},{6,4},{7,31},{8,10},{9,17},... | collective-permute-start | bytes 393224 | tf_op jit(solution)/shard_map/ppermute | solution.py:276
  7.6 5.0 %collective-permute-start.2 = (bf16[32,2048]{1,0:T(8,128)(2,1)S(1)}, bf16[32,2048]{1,0:T(8,128)(2,1)S(1)}, u32[]{:S(2)}, u32[]{:S(2)}) collective-permute-start(bf16[32,2048]{1,0:T(8,128)(2,1)S(1)} %get-tuple-element.15), channel_id=1, source_target_pairs={{0,4},{1,9},{2,6},{3,11},{4,0},{5,13},{6,2},{7,15},{8,12},{9,1},{1... | collective-permute-start | bytes 393224 | tf_op jit(solution)/shard_map/ppermute | solution.py:276
  7.7 12.9 %collective-permute-start.8 = (f32[3,8,2048]{2,1,0:T(8,128)S(1)}, f32[3,8,2048]{2,1,0:T(8,128)S(1)}, u32[]{:S(2)}, u32[]{:S(2)}) collective-permute-start(f32[3,8,2048]{2,1,0:T(8,128)S(1)} %pack.1), channel_id=1, source_target_pairs={{0,1},{1,0},{2,3},{3,2},{4,5},{5,4},{6,7},{7,6},{8,9},{9,8},{10,11... | collective-permute-start | bytes 589832 | tf_op jit(solution)/shard_map/ppermute | solution.py:256
  12.7 6.1 %collective-permute-start.3 = (f32[8,2048]{1,0:T(8,128)S(1)}, f32[8,2048]{1,0:T(8,128)S(1)}, u32[]{:S(2)}, u32[]{:S(2)}) collective-permute-start(f32[8,2048]{1,0:T(8,128)S(1)} %get-tuple-element.17), channel_id=1, source_target_pairs={{0,16},{1,7},{2,18},{3,5},{4,20},{5,3},{6,22},{7,1},{8,24},{9,15},... | collective-permute-start | bytes 196616 | tf_op jit(solution)/shard_map/ppermute | solution.py:276
  15.3 5.2 %collective-permute-start.4 = (f32[8,2048]{1,0:T(8,128)S(1)}, f32[8,2048]{1,0:T(8,128)S(1)}, u32[]{:S(2)}, u32[]{:S(2)}) collective-permute-start(f32[8,2048]{1,0:T(8,128)S(1)} %get-tuple-element.18), channel_id=1, source_target_pairs={{0,24},{1,3},{2,26},{3,1},{4,28},{5,7},{6,30},{7,5},{8,16},{9,11},... | collective-permute-start | bytes 196616 | tf_op jit(solution)/shard_map/ppermute | solution.py:276
  16.5 4.7 %collective-permute-start.5 = (f32[8,2304]{1,0:T(8,128)S(1)}, f32[8,2304]{1,0:T(8,128)S(1)}, u32[]{:S(2)}, u32[]{:S(2)}) collective-permute-start(f32[8,2304]{1,0:T(8,128)S(1)} %get-tuple-element.19), channel_id=1, source_target_pairs={{0,8},{1,5},{2,10},{3,7},{4,12},{5,1},{6,14},{7,3},{8,0},{9,13},{1... | collective-permute-start | bytes 221192 | tf_op jit(solution)/shard_map/ppermute | solution.py:276
  16.9 4.4 %collective-permute-start.7 = (f32[8,2304]{1,0:T(8,128)S(1)}, f32[8,2304]{1,0:T(8,128)S(1)}, u32[]{:S(2)}, u32[]{:S(2)}) collective-permute-start(f32[8,2304]{1,0:T(8,128)S(1)} %get-tuple-element.19), channel_id=1, source_target_pairs={{0,9},{1,4},{2,11},{3,6},{4,13},{5,0},{6,15},{7,2},{8,1},{9,12},{1... | collective-permute-start | bytes 221192 | tf_op jit(solution)/shard_map/ppermute | solution.py:276
  20.5 1.3 %collective-permute-start.6 = (f32[8,2048]{1,0:T(8,128)S(1)}, f32[8,2048]{1,0:T(8,128)S(1)}, u32[]{:S(2)}, u32[]{:S(2)}) collective-permute-start(f32[8,2048]{1,0:T(8,128)S(1)} %partial.1.part), channel_id=1, source_target_pairs={{0,1},{1,0},{2,3},{3,2},{4,5},{5,4},{6,7},{7,6},{8,9},{9,8},{10,11... | collective-permute-start | bytes 196616 | tf_op jit(solution)/shard_map/ppermute | solution.py:256

commit v6 on v5

--- a/solution.py
+++ b/solution.py
@@ -216,6 +216,11 @@
     outs, published, (held, rounded, sems) = refs[:3], refs[3], refs[4:]
     copies = []
     ours = stepped(part[...] + last[:, : part.shape[1]], first, second, master, step)
+    for k, value in enumerate(ours):
+        held[k] = value
+        copy = pltpu.make_async_copy(held.at[k], outs[k].at[0], sems.at[k])
+        copy.start()
+        copies.append(copy)
     ff = part.shape[1]
     steps = [far_last[:, ff + k * 128 : ff + k * 128 + 1] for k in range(2)]
     theirs = stepped(far_part[...] + far_last[:, :ff], far.at[0:1], far.at[1:2], far.at[2:3], steps)[0]
@@ -223,12 +228,7 @@
     rounded[0] = jnp.where(here, ours[0], theirs).astype(jnp.bfloat16)
     rounded[1] = jnp.where(here, theirs, ours[0]).astype(jnp.bfloat16)
     copies.append(pltpu.make_async_copy(rounded, published, sems.at[3]))
-    copies[0].start()
-    for k, value in enumerate(ours):
-        held[k] = value
-        copy = pltpu.make_async_copy(held.at[k], outs[k].at[0], sems.at[k])
-        copy.start()
-        copies.append(copy)
+    copies[-1].start()
     for copy in copies:
         copy.wait()
 

time: 22.9 us -> 22.8 us (level)
  no operation moved by 1% of the time
where the time goes in v6:
time: 22.8 us; the launch traced here: 22.7 us
  starting transfers between devices  9.3 us (41%)
  waiting for transfers between devices  8.43 us (37%)
  Pallas kernels  3.39 us (15%)
  between operations  1.43 us (6%)
    ppermute x7, starting transfers between devices, exchange(): return lax.ppermute(block, ('dp', 'rollout'), pairs)  8.8 us
    ppermute x7, waiting for transfers between devices, exchange(): return lax.ppermute(block, ('dp', 'rollout'), pairs)  7.85 us
    pallas_call x1, Pallas kernels, product_blocks(): pl.pallas_call(functools.partial(product_kernel, inner, outer, cuts), out...  2.43 us
    pallas_call x1, Pallas kernels, finished(): pl.pallas_call(finish_kernel, out_shape=[jax.ShapeDtypeStruct(shape, jnp....  0.84 us
    ppermute x2, waiting for transfers between devices, over_cores(): return lax.ppermute(x, 'rollout', [(0, 1), (1, 0)])  0.58 us
    ppermute x2, starting transfers between devices, over_cores(): return lax.ppermute(x, 'rollout', [(0, 1), (1, 0)])  0.5 us
  transfers between devices with their start and end apart: 9, of which 7 were waited for; matrix products, arithmetic and copies ran while one was open for 0% of the time, Pallas kernels for 1%

profile of v6, /device:TPU:0, one launch (start us, length us, event | category | flops | bytes accessed | tf_op | source)
XLA Modules:
  0.0 22.7 jit_solution(15974119244682423220)
XLA Ops:
  0.6 0.0 copy-start.4
  0.7 2.4 %product.1 = (bf16[32,2048]{1,0:T(8,128)(2,1)S(1)}, bf16[32,2048]{1,0:T(8,128)(2,1)S(1)}, bf16[32,2048]{1,0:T(8,128)(2,1)S(1)}, bf16[32,2048]{1,0:T(8,128)(2,1)S(1)}) custom-call(bf16[768,128]{1,0:T(8,128)(2,1)} %bitcast.9, bf16[768,2048]{1,0:T(8,128)(2,1)} %bitcast.8), custom_call_target="tpu_custom_call" | custom-call | tf_op jit(solution)/shard_map/product/pallas_call | solution.py:69
  3.1 3.9 %collective-permute-start = (bf16[32,2048]{1,0:T(8,128)(2,1)S(1)}, bf16[32,2048]{1,0:T(8,128)(2,1)S(1)}, u32[]{:S(2)}, u32[]{:S(2)}) collective-permute-start(bf16[32,2048]{1,0:T(8,128)(2,1)S(1)} %get-tuple-element.13), channel_id=1, source_target_pairs={{0,6},{1,17},{2,4},{3,19},{4,2},{5,21},{6,0},{7,23},{8,14},{9,25},... | collective-permute-start | bytes 393224 | tf_op jit(solution)/shard_map/ppermute | solution.py:276
  7.1 0.5 %collective-permute-start.1 = (bf16[32,2048]{1,0:T(8,128)(2,1)S(1)}, bf16[32,2048]{1,0:T(8,128)(2,1)S(1)}, u32[]{:S(2)}, u32[]{:S(2)}) collective-permute-start(bf16[32,2048]{1,0:T(8,128)(2,1)S(1)} %get-tuple-element.14), channel_id=1, source_target_pairs={{0,2},{1,25},{2,0},{3,27},{4,6},{5,29},{6,4},{7,31},{8,10},{9,17},... | collective-permute-start | bytes 393224 | tf_op jit(solution)/shard_map/ppermute | solution.py:276
  7.6 0.1 collective-permute-start.2
  7.7 0.0 copy-done
  7.7 0.4 %collective-permute-start.8 = (f32[3,8,2048]{2,1,0:T(8,128)S(1)}, f32[3,8,2048]{2,1,0:T(8,128)S(1)}, u32[]{:S(2)}, u32[]{:S(2)}) collective-permute-start(f32[3,8,2048]{2,1,0:T(8,128)S(1)} %pack.1), channel_id=1, source_target_pairs={{0,1},{1,0},{2,3},{3,2},{4,5},{5,4},{6,7},{7,6},{8,9},{9,8},{10,11... | collective-permute-start | bytes 589832 | tf_op jit(solution)/shard_map/ppermute | solution.py:256
  8.8 0.1 copy.12.refs_4_.step
  8.9 1.1 %collective-permute-done.refs_1_ = bf16[32,2048]{1,0:T(8,128)(2,1)S(1)} collective-permute-done((bf16[32,2048]{1,0:T(8,128)(2,1)S(1)}, bf16[32,2048]{1,0:T(8,128)(2,1)S(1)}, u32[]{:S(2)}, u32[]{:S(2)}) %collective-permute-start) | collective-permute-done | bytes 131104 | tf_op jit(solution)/shard_map/ppermute | solution.py:276
  10.0 2.0 %collective-permute-done.1.refs_2_ = bf16[32,2048]{1,0:T(8,128)(2,1)S(1)} collective-permute-done((bf16[32,2048]{1,0:T(8,128)(2,1)S(1)}, bf16[32,2048]{1,0:T(8,128)(2,1)S(1)}, u32[]{:S(2)}, u32[]{:S(2)}) %collective-permute-start.1) | collective-permute-done | bytes 131104 | tf_op jit(solution)/shard_map/ppermute | solution.py:276
  12.0 0.5 %collective-permute-done.2.refs_3_ = bf16[32,2048]{1,0:T(8,128)(2,1)S(1)} collective-permute-done((bf16[32,2048]{1,0:T(8,128)(2,1)S(1)}, bf16[32,2048]{1,0:T(8,128)(2,1)S(1)}, u32[]{:S(2)}, u32[]{:S(2)}) %collective-permute-start.2) | collective-permute-done | bytes 131104 | tf_op jit(solution)/shard_map/ppermute | solution.py:276
  12.6 0.1 middle.1
  12.7 2.6 %collective-permute-start.3 = (f32[8,2048]{1,0:T(8,128)S(1)}, f32[8,2048]{1,0:T(8,128)S(1)}, u32[]{:S(2)}, u32[]{:S(2)}) collective-permute-start(f32[8,2048]{1,0:T(8,128)S(1)} %get-tuple-element.17), channel_id=1, source_target_pairs={{0,16},{1,7},{2,18},{3,5},{4,20},{5,3},{6,22},{7,1},{8,24},{9,15},... | collective-permute-start | bytes 196616 | tf_op jit(solution)/shard_map/ppermute | solution.py:276
  15.3 1.2 %collective-permute-start.4 = (f32[8,2048]{1,0:T(8,128)S(1)}, f32[8,2048]{1,0:T(8,128)S(1)}, u32[]{:S(2)}, u32[]{:S(2)}) collective-permute-start(f32[8,2048]{1,0:T(8,128)S(1)} %get-tuple-element.18), channel_id=1, source_target_pairs={{0,24},{1,3},{2,26},{3,1},{4,28},{5,7},{6,30},{7,5},{8,16},{9,11},... | collective-permute-start | bytes 196616 | tf_op jit(solution)/shard_map/ppermute | solution.py:276
  16.5 0.3 %collective-permute-start.5 = (f32[8,2304]{1,0:T(8,128)S(1)}, f32[8,2304]{1,0:T(8,128)S(1)}, u32[]{:S(2)}, u32[]{:S(2)}) collective-permute-start(f32[8,2304]{1,0:T(8,128)S(1)} %get-tuple-element.19), channel_id=1, source_target_pairs={{0,8},{1,5},{2,10},{3,7},{4,12},{5,1},{6,14},{7,3},{8,0},{9,13},{1... | collective-permute-start | bytes 221192 | tf_op jit(solution)/shard_map/ppermute | solution.py:276
  16.9 0.0 collective-permute-start.7
  16.9 1.9 %collective-permute-done.3.refs_1_ = f32[8,2048]{1,0:T(8,128)S(1)} collective-permute-done((f32[8,2048]{1,0:T(8,128)S(1)}, f32[8,2048]{1,0:T(8,128)S(1)}, u32[]{:S(2)}, u32[]{:S(2)}) %collective-permute-start.3) | collective-permute-done | bytes 65568 | tf_op jit(solution)/shard_map/ppermute | solution.py:276
  18.8 1.7 %collective-permute-done.4.refs_2_ = f32[8,2048]{1,0:T(8,128)S(1)} collective-permute-done((f32[8,2048]{1,0:T(8,128)S(1)}, f32[8,2048]{1,0:T(8,128)S(1)}, u32[]{:S(2)}, u32[]{:S(2)}) %collective-permute-start.4) | collective-permute-done | bytes 65568 | tf_op jit(solution)/shard_map/ppermute | solution.py:276
  20.5 0.1 collective-permute-start.6
  20.7 0.0 collective-permute-done.8.far
  20.7 0.6 %collective-permute-done.5.last = f32[8,2304]{1,0:T(8,128)S(1)} collective-permute-done((f32[8,2304]{1,0:T(8,128)S(1)}, f32[8,2304]{1,0:T(8,128)S(1)}, u32[]{:S(2)}, u32[]{:S(2)}) %collective-permute-start.5) | collective-permute-done | bytes 73760 | tf_op jit(solution)/shard_map/ppermute | solution.py:276
  21.3 0.0 collective-permute-done.7.far_last
  21.3 0.6 %collective-permute-done.6.far_part = f32[8,2048]{1,0:T(8,128)S(1)} collective-permute-done((f32[8,2048]{1,0:T(8,128)S(1)}, f32[8,2048]{1,0:T(8,128)S(1)}, u32[]{:S(2)}, u32[]{:S(2)}) %collective-permute-start.6) | collective-permute-done | bytes 65568 | tf_op jit(solution)/shard_map/ppermute | solution.py:256
  21.8 0.8 %finish.1 = (f32[1,8,2048]{2,1,0:T(8,128)}, f32[1,8,2048]{2,1,0:T(8,128)}, f32[1,8,2048]{2,1,0:T(8,128)}, bf16[2,8,2048]{2,1,0:T(8,128)(2,1)}) custom-call(f32[8,2048]{1,0:T(8,128)S(1)} %partial.1.part, f32[8,2304]{1,0:T(8,128)S(1)} %collective-permute-done.5.last, f32[8,2048]{1,0:T(8,128)S(1)} %collective-permute-done.6.far_part, ...), custom_call_target="tpu_custom_call" | custom-call | tf_op jit(solution)/shard_map/finish/pallas_call | solution.py:239
  (11 shorter events, 0.1 us)
Async XLA Ops:
  0.6 8.2 %copy-start.4 = (f32[2]{0:T(128)S(1)}, f32[2]{0:T(128)}, u32[]{:S(2)}) copy-start(f32[2]{0:T(128)} %constant.10.clone) | copy-start | bytes 28
  0.6 7.1 %copy-start.2 = (f32[1,8,2048]{2,1,0:T(8,128)S(1)}, f32[1,8,2048]{2,1,0:T(8,128)}, u32[]{:S(2)}) copy-start(f32[1,8,2048]{2,1,0:T(8,128)} %master.3) | copy-start | bytes 196612
  0.7 7.0 %copy-start = (f32[1,8,2048]{2,1,0:T(8,128)S(1)}, f32[1,8,2048]{2,1,0:T(8,128)}, u32[]{:S(2)}) copy-start(f32[1,8,2048]{2,1,0:T(8,128)} %first.3) | copy-start | bytes 196612
  0.7 7.0 %copy-start.1 = (f32[1,8,2048]{2,1,0:T(8,128)S(1)}, f32[1,8,2048]{2,1,0:T(8,128)}, u32[]{:S(2)}) copy-start(f32[1,8,2048]{2,1,0:T(8,128)} %second.3) | copy-start | bytes 196612
  0.7 19.9 %copy-start.3 = (s32[2]{0:T(128)S(1)}, s32[2]{0:T(128)}, u32[]{:S(2)}) copy-start(s32[2]{0:T(128)} %param.14) | copy-start | bytes 28
  3.1 6.9 %collective-permute-start = (bf16[32,2048]{1,0:T(8,128)(2,1)S(1)}, bf16[32,2048]{1,0:T(8,128)(2,1)S(1)}, u32[]{:S(2)}, u32[]{:S(2)}) collective-permute-start(bf16[32,2048]{1,0:T(8,128)(2,1)S(1)} %get-tuple-element.13), channel_id=1, source_target_pairs={{0,6},{1,17},{2,4},{3,19},{4,2},{5,21},{6,0},{7,23},{8,14},{9,25},... | collective-permute-start | bytes 393224 | tf_op jit(solution)/shard_map/ppermute | solution.py:276
  7.1 5.0 %collective-permute-start.1 = (bf16[32,2048]{1,0:T(8,128)(2,1)S(1)}, bf16[32,2048]{1,0:T(8,128)(2,1)S(1)}, u32[]{:S(2)}, u32[]{:S(2)}) collective-permute-start(bf16[32,2048]{1,0:T(8,128)(2,1)S(1)} %get-tuple-element.14), channel_id=1, source_target_pairs={{0,2},{1,25},{2,0},{3,27},{4,6},{5,29},{6,4},{7,31},{8,10},{9,17},... | collective-permute-start | bytes 393224 | tf_op jit(solution)/shard_map/ppermute | solution.py:276
  7.6 5.0 %collective-permute-start.2 = (bf16[32,2048]{1,0:T(8,128)(2,1)S(1)}, bf16[32,2048]{1,0:T(8,128)(2,1)S(1)}, u32[]{:S(2)}, u32[]{:S(2)}) collective-permute-start(bf16[32,2048]{1,0:T(8,128)(2,1)S(1)} %get-tuple-element.15), channel_id=1, source_target_pairs={{0,4},{1,9},{2,6},{3,11},{4,0},{5,13},{6,2},{7,15},{8,12},{9,1},{1... | collective-permute-start | bytes 393224 | tf_op jit(solution)/shard_map/ppermute | solution.py:276
  7.7 12.9 %collective-permute-start.8 = (f32[3,8,2048]{2,1,0:T(8,128)S(1)}, f32[3,8,2048]{2,1,0:T(8,128)S(1)}, u32[]{:S(2)}, u32[]{:S(2)}) collective-permute-start(f32[3,8,2048]{2,1,0:T(8,128)S(1)} %pack.1), channel_id=1, source_target_pairs={{0,1},{1,0},{2,3},{3,2},{4,5},{5,4},{6,7},{7,6},{8,9},{9,8},{10,11... | collective-permute-start | bytes 589832 | tf_op jit(solution)/shard_map/ppermute | solution.py:256
  12.7 6.1 %collective-permute-start.3 = (f32[8,2048]{1,0:T(8,128)S(1)}, f32[8,2048]{1,0:T(8,128)S(1)}, u32[]{:S(2)}, u32[]{:S(2)}) collective-permute-start(f32[8,2048]{1,0:T(8,128)S(1)} %get-tuple-element.17), channel_id=1, source_target_pairs={{0,16},{1,7},{2,18},{3,5},{4,20},{5,3},{6,22},{7,1},{8,24},{9,15},... | collective-permute-start | bytes 196616 | tf_op jit(solution)/shard_map/ppermute | solution.py:276
  15.3 5.2 %collective-permute-start.4 = (f32[8,2048]{1,0:T(8,128)S(1)}, f32[8,2048]{1,0:T(8,128)S(1)}, u32[]{:S(2)}, u32[]{:S(2)}) collective-permute-start(f32[8,2048]{1,0:T(8,128)S(1)} %get-tuple-element.18), channel_id=1, source_target_pairs={{0,24},{1,3},{2,26},{3,1},{4,28},{5,7},{6,30},{7,5},{8,16},{9,11},... | collective-permute-start | bytes 196616 | tf_op jit(solution)/shard_map/ppermute | solution.py:276
  16.5 4.7 %collective-permute-start.5 = (f32[8,2304]{1,0:T(8,128)S(1)}, f32[8,2304]{1,0:T(8,128)S(1)}, u32[]{:S(2)}, u32[]{:S(2)}) collective-permute-start(f32[8,2304]{1,0:T(8,128)S(1)} %get-tuple-element.19), channel_id=1, source_target_pairs={{0,8},{1,5},{2,10},{3,7},{4,12},{5,1},{6,14},{7,3},{8,0},{9,13},{1... | collective-permute-start | bytes 221192 | tf_op jit(solution)/shard_map/ppermute | solution.py:276
  16.9 4.4 %collective-permute-start.7 = (f32[8,2304]{1,0:T(8,128)S(1)}, f32[8,2304]{1,0:T(8,128)S(1)}, u32[]{:S(2)}, u32[]{:S(2)}) collective-permute-start(f32[8,2304]{1,0:T(8,128)S(1)} %get-tuple-element.19), channel_id=1, source_target_pairs={{0,9},{1,4},{2,11},{3,6},{4,13},{5,0},{6,15},{7,2},{8,1},{9,12},{1... | collective-permute-start | bytes 221192 | tf_op jit(solution)/shard_map/ppermute | solution.py:276
  20.5 1.3 %collective-permute-start.6 = (f32[8,2048]{1,0:T(8,128)S(1)}, f32[8,2048]{1,0:T(8,128)S(1)}, u32[]{:S(2)}, u32[]{:S(2)}) collective-permute-start(f32[8,2048]{1,0:T(8,128)S(1)} %partial.1.part), channel_id=1, source_target_pairs={{0,1},{1,0},{2,3},{3,2},{4,5},{5,4},{6,7},{7,6},{8,9},{9,8},{10,11... | collective-permute-start | bytes 196616 | tf_op jit(solution)/shard_map/ppermute | solution.py:256
